TPU v7x, 32 devices: a whole 2x2x4 slice. The times are simulated.
32 devices in a mesh: sec: 8 (over y, x, core), tile: 4 (over z).
Axes of the slice: x: 2, y: 2, z: 4, core: 2. Of those that a mesh axis runs over, the one named last changes fastest.
Arguments:
- in_plane_force: float32 [2, 16, 256, 256], P(None, 'sec', 'tile'), may hold values from -6 to 6
- stiffness: float32 [16, 256, 256], P('sec', 'tile'), may hold values from 0.5 to 2
- stiffness_z: float32 [16, 256, 256], P(None, ('tile', 'sec')), may hold values from 0.3 to 1.5
- patch_dest: int32 [8, 4, 256, 1], P('sec', 'tile'), may hold values from 0 to 7; in each aligned block of 256 rows (0 to 255, 256 to 511, ..., all dimensions but the last counted through in order) at most 64 rows name the same one
- patch_pos: int32 [8, 4, 256], P('sec', 'tile'), may hold values from 0 to 31
- patch_flow: float32 [8, 4, 256, 2, 128], P('sec', 'tile'), may hold values from -6 to 6
- patch_conf: float32 [8, 4, 256, 128], P('sec', 'tile'), may hold values from 0.2 to 1
Outputs:
- displacement: float32 [2, 16, 256, 256], P(None, None, ('tile', 'sec'))
Inputs may be any that keep to these rules, and one draw needn't show every extreme that they name: `patch_dest`: among the 256 patches of one section group and tile, at most 64 name the same owner; in some of them an owner is named exactly 64 times.
All inputs are finite; a program needn't handle non-finite values.
Results may differ from a plain program's by a relative error of at most 0.00002.
Values sent between devices are 32-bit elements; how exact they have to be, the bound alone decides.
No kernel may reach another device: no remote copies, remote signals or barrier semaphores. Data moves between devices by JAX's collectives and lax.ppermute only.
A program may use at most 64 MiB of HBM per device.

v0:
```python
import jax
import jax.numpy as jnp
from jax import lax
from jax.sharding import PartitionSpec as P

ISTEPS = 8
ZSTEPS = 8


STEP_PLANE = 0.12
STEP_CROSS = 0.15


def padded(shard, sides, width):
    for axis, dim in sides:
        count, length = (lax.axis_size(axis), shard.shape[dim])
        up = [(i, (i + 1) % count) for i in range(count - 1)]
        down = [(j, i) for i, j in up]
        last = lax.slice_in_dim(shard, length - width, length, axis=dim)
        leading = lax.slice_in_dim(shard, 0, width, axis=dim)
        before = lax.ppermute(last, axis, up)
        after = lax.ppermute(leading, axis, down)
        shard = jnp.concatenate([before, shard, after], axis=dim)
    return shard


def plane_step(extended, force, stiff):
    centre = extended[:, :, 1:-1]
    zero_column = jnp.zeros(centre.shape[:-1] + (1,), jnp.float32)
    left = jnp.concatenate([zero_column, centre[..., :-1]], axis=-1)
    right = jnp.concatenate([centre[..., 1:], zero_column], axis=-1)
    laplace = extended[:, :, 2:] + extended[:, :, :-2] + right + left - 4.0 * centre
    return centre + STEP_PLANE * (stiff * laplace + force)


def cross_steps(field, pull, weight, stiffness_z):
    for step in range(ZSTEPS):
        zero_layer = jnp.zeros(field.shape[:1] + (1,) + field.shape[2:], jnp.float32)
        below = jnp.concatenate([zero_layer, field[:, :-1]], axis=1)
        above = jnp.concatenate([field[:, 1:], zero_layer], axis=1)
        stretch = pull - weight[None] * (field - below)
        stretch_above = jnp.concatenate([stretch[:, 1:], zero_layer], axis=1)
        field = field + STEP_CROSS * (
            stiffness_z[None] * (above + below - 2.0 * field) + stretch - stretch_above
        )
    return field


def spread(target, payload, layers, rows, blocks):
    width = payload.shape[2]
    grid = jnp.zeros((layers * rows * blocks, 3, width), jnp.float32).at[target].add(payload)
    grid = grid.reshape(layers, rows, blocks, 3, width).transpose(3, 0, 1, 2, 4)
    return grid.reshape(3, layers, rows, blocks * width)


def per_device(
    in_plane_force, stiffness, stiffness_z, patch_dest, patch_pos, patch_flow, patch_conf
):
    groups = lax.axis_size("sec")
    layers, rows, columns = stiffness.shape
    inner_rows = rows // groups
    width = patch_flow.shape[-1]
    blocks = columns // width
    count = patch_pos.shape[2]
    field = STEP_PLANE * in_plane_force
    for step in range(1, ISTEPS):
        extended = padded(field, (("tile", 2),), 1)
        field = plane_step(extended, in_plane_force, stiffness[None])
    owner = patch_dest.reshape(count)
    place = patch_pos.reshape(count)
    layer = place // (inner_rows * blocks)
    inner_row = place // blocks % inner_rows
    column_block = place % blocks
    confidence = patch_conf.reshape(count, width)
    flow = patch_flow.reshape(count, 2, width)
    payload = jnp.concatenate([confidence[:, None, :] * flow, confidence[:, None, :]], axis=1)
    target = (layer * rows + owner * inner_rows + inner_row) * blocks + column_block
    local_forces = spread(target, payload, layers, rows, blocks)
    stacked = jnp.concatenate([field, local_forces], axis=0)
    moved_all = lax.all_to_all(stacked, "sec", split_axis=2, concat_axis=1, tiled=True)
    moved = moved_all[:2]
    forces = moved_all[2:]
    return cross_steps(moved, forces[:2], forces[2], stiffness_z)


def solution(mesh):
    placed = (
        P(None, "sec", "tile", None),
        P("sec", "tile", None),
        P(None, ("tile", "sec"), None),
        P("sec", "tile", None, None),
        P("sec", "tile", None),
        P("sec", "tile", None, None, None),
        P("sec", "tile", None, None),
    )
    return jax.shard_map(
        per_device,
        mesh=mesh,
        in_specs=placed,
        out_specs=P(None, None, ("tile", "sec"), None),
        check_vma=False,
    )
```

profile of v0, /device:TPU:0, one launch (start us, length us, event | category | flops | bytes accessed | tf_op | source)
XLA Modules:
  0.0 88.1 jit_solution(2244491538358134928)
XLA Ops:
  0.0 1.0 %broadcast_multiply_fusion = f32[2,2,64,256]{3,2,1,0:T(8,128)S(1)} fusion(f32[2,2,64,256]{3,2,1,0:T(8,128)} %param.7), kind=kLoop, calls=%fused_computation.92 | loop fusion | flops 65536 | bytes 524288 | tf_op jit(solution)/shard_map/mul | solution.py:65
  1.0 4.9 %collective-permute-start.1 = (f32[2,2,1,256]{3,2,1,0:T(1,128)S(1)}, f32[2,2,1,256]{3,2,1,0:T(1,128)S(1)}, u32[]{:S(2)}, u32[]{:S(2)}) collective-permute-start(f32[2,2,1,256]{3,2,1,0:T(1,128)S(1)} %get-tuple-element.50), channel_id=1, source_target_pairs={{0,1},{1,2},{2,3},{4,5},{5,6},{6,7},{8,9},{9,10},{10,11},{12,13},{... | collective-permute-start | bytes 12296 | tf_op jit(solution)/shard_map/ppermute | solution.py:21
  6.0 1.4 %collective-permute-start = (f32[2,2,1,256]{3,2,1,0:T(1,128)S(1)}, f32[2,2,1,256]{3,2,1,0:T(1,128)S(1)}, u32[]{:S(2)}, u32[]{:S(2)}) collective-permute-start(f32[2,2,1,256]{3,2,1,0:T(1,128)S(1)} %get-tuple-element.49), channel_id=1, source_target_pairs={{1,0},{2,1},{3,2},{5,4},{6,5},{7,6},{9,8},{10,9},{11,10},{13,12},{... | collective-permute-start | bytes 12296 | tf_op jit(solution)/shard_map/ppermute | solution.py:22
  7.4 0.1 fusion.80
  7.6 0.1 bitcast_multiply_fusion
  7.8 0.2 pad_maximum_fusion.1
  8.1 8.4 %scatter_fusion = f32[256,3,128]{2,1,0:T(4,128)S(1)} fusion(f32[256,3,128]{2,1,0:T(4,128)S(1)} %broadcast_in_dim.2, s32[256]{0:T(256)S(1)} %bitcast.68, f32[256,3,128]{2,1,0:T(4,128)S(1)} %pad_maximum_fusion.1), kind=kCustom, calls=%fused_computation | custom fusion | flops 98304 | bytes 1180672 | tf_op jit(solution)/shard_map/scatter-add | solution.py:51
  16.4 0.2 copy.25
  16.7 0.3 reshape.218
  17.0 0.6 copy-done
  17.6 0.2 fusion.55
  17.8 4.5 %collective-permute-start.3 = (f32[2,2,1,256]{3,2,1,0:T(1,128)S(1)}, f32[2,2,1,256]{3,2,1,0:T(1,128)S(1)}, u32[]{:S(2)}, u32[]{:S(2)}) collective-permute-start(f32[2,2,1,256]{3,2,1,0:T(1,128)S(1)} %get-tuple-element.46), channel_id=1, source_target_pairs={{0,1},{1,2},{2,3},{4,5},{5,6},{6,7},{8,9},{9,10},{10,11},{12,13},{... | collective-permute-start | bytes 12296 | tf_op jit(solution)/shard_map/ppermute | solution.py:21
  22.4 1.3 %collective-permute-start.2 = (f32[2,2,1,256]{3,2,1,0:T(1,128)S(1)}, f32[2,2,1,256]{3,2,1,0:T(1,128)S(1)}, u32[]{:S(2)}, u32[]{:S(2)}) collective-permute-start(f32[2,2,1,256]{3,2,1,0:T(1,128)S(1)} %get-tuple-element.45), channel_id=1, source_target_pairs={{1,0},{2,1},{3,2},{5,4},{6,5},{7,6},{9,8},{10,9},{11,10},{13,12},{... | collective-permute-start | bytes 12296 | tf_op jit(solution)/shard_map/ppermute | solution.py:22
  23.7 0.1 fusion.78
  23.8 4.1 %collective-permute-done.2 = f32[2,2,1,256]{3,2,1,0:T(1,128)S(1)} collective-permute-done((f32[2,2,1,256]{3,2,1,0:T(1,128)S(1)}, f32[2,2,1,256]{3,2,1,0:T(1,128)S(1)}, u32[]{:S(2)}, u32[]{:S(2)}) %collective-permute-start.2) | collective-permute-done | bytes 4128 | tf_op jit(solution)/shard_map/ppermute | solution.py:22
  27.9 0.2 fusion.47
  28.1 3.5 %collective-permute-start.5 = (f32[2,2,1,256]{3,2,1,0:T(1,128)S(1)}, f32[2,2,1,256]{3,2,1,0:T(1,128)S(1)}, u32[]{:S(2)}, u32[]{:S(2)}) collective-permute-start(f32[2,2,1,256]{3,2,1,0:T(1,128)S(1)} %get-tuple-element.42), channel_id=1, source_target_pairs={{0,1},{1,2},{2,3},{4,5},{5,6},{6,7},{8,9},{9,10},{10,11},{12,13},{... | collective-permute-start | bytes 12296 | tf_op jit(solution)/shard_map/ppermute | solution.py:21
  31.5 1.3 %collective-permute-start.4 = (f32[2,2,1,256]{3,2,1,0:T(1,128)S(1)}, f32[2,2,1,256]{3,2,1,0:T(1,128)S(1)}, u32[]{:S(2)}, u32[]{:S(2)}) collective-permute-start(f32[2,2,1,256]{3,2,1,0:T(1,128)S(1)} %get-tuple-element.41), channel_id=1, source_target_pairs={{1,0},{2,1},{3,2},{5,4},{6,5},{7,6},{9,8},{10,9},{11,10},{13,12},{... | collective-permute-start | bytes 12296 | tf_op jit(solution)/shard_map/ppermute | solution.py:22
  32.8 0.1 fusion.76
  33.0 4.1 %collective-permute-done.4 = f32[2,2,1,256]{3,2,1,0:T(1,128)S(1)} collective-permute-done((f32[2,2,1,256]{3,2,1,0:T(1,128)S(1)}, f32[2,2,1,256]{3,2,1,0:T(1,128)S(1)}, u32[]{:S(2)}, u32[]{:S(2)}) %collective-permute-start.4) | collective-permute-done | bytes 4128 | tf_op jit(solution)/shard_map/ppermute | solution.py:22
  37.0 0.2 fusion.39
  37.2 3.5 %collective-permute-start.7 = (f32[2,2,1,256]{3,2,1,0:T(1,128)S(1)}, f32[2,2,1,256]{3,2,1,0:T(1,128)S(1)}, u32[]{:S(2)}, u32[]{:S(2)}) collective-permute-start(f32[2,2,1,256]{3,2,1,0:T(1,128)S(1)} %get-tuple-element.38), channel_id=1, source_target_pairs={{0,1},{1,2},{2,3},{4,5},{5,6},{6,7},{8,9},{9,10},{10,11},{12,13},{... | collective-permute-start | bytes 12296 | tf_op jit(solution)/shard_map/ppermute | solution.py:21
  40.7 1.3 %collective-permute-start.6 = (f32[2,2,1,256]{3,2,1,0:T(1,128)S(1)}, f32[2,2,1,256]{3,2,1,0:T(1,128)S(1)}, u32[]{:S(2)}, u32[]{:S(2)}) collective-permute-start(f32[2,2,1,256]{3,2,1,0:T(1,128)S(1)} %get-tuple-element.37), channel_id=1, source_target_pairs={{1,0},{2,1},{3,2},{5,4},{6,5},{7,6},{9,8},{10,9},{11,10},{13,12},{... | collective-permute-start | bytes 12296 | tf_op jit(solution)/shard_map/ppermute | solution.py:22
  42.0 0.1 fusion.74
  42.2 4.1 %collective-permute-done.6 = f32[2,2,1,256]{3,2,1,0:T(1,128)S(1)} collective-permute-done((f32[2,2,1,256]{3,2,1,0:T(1,128)S(1)}, f32[2,2,1,256]{3,2,1,0:T(1,128)S(1)}, u32[]{:S(2)}, u32[]{:S(2)}) %collective-permute-start.6) | collective-permute-done | bytes 4128 | tf_op jit(solution)/shard_map/ppermute | solution.py:22
  46.2 0.2 fusion.31
  46.4 1.9 %collective-permute-start.9 = (f32[2,2,1,256]{3,2,1,0:T(1,128)S(1)}, f32[2,2,1,256]{3,2,1,0:T(1,128)S(1)}, u32[]{:S(2)}, u32[]{:S(2)}) collective-permute-start(f32[2,2,1,256]{3,2,1,0:T(1,128)S(1)} %get-tuple-element.34), channel_id=1, source_target_pairs={{0,1},{1,2},{2,3},{4,5},{5,6},{6,7},{8,9},{9,10},{10,11},{12,13},{... | collective-permute-start | bytes 12296 | tf_op jit(solution)/shard_map/ppermute | solution.py:21
  48.3 1.3 %collective-permute-start.8 = (f32[2,2,1,256]{3,2,1,0:T(1,128)S(1)}, f32[2,2,1,256]{3,2,1,0:T(1,128)S(1)}, u32[]{:S(2)}, u32[]{:S(2)}) collective-permute-start(f32[2,2,1,256]{3,2,1,0:T(1,128)S(1)} %get-tuple-element.33), channel_id=1, source_target_pairs={{1,0},{2,1},{3,2},{5,4},{6,5},{7,6},{9,8},{10,9},{11,10},{13,12},{... | collective-permute-start | bytes 12296 | tf_op jit(solution)/shard_map/ppermute | solution.py:22
  49.6 0.1 fusion.72
  49.8 4.1 %collective-permute-done.8 = f32[2,2,1,256]{3,2,1,0:T(1,128)S(1)} collective-permute-done((f32[2,2,1,256]{3,2,1,0:T(1,128)S(1)}, f32[2,2,1,256]{3,2,1,0:T(1,128)S(1)}, u32[]{:S(2)}, u32[]{:S(2)}) %collective-permute-start.8) | collective-permute-done | bytes 4128 | tf_op jit(solution)/shard_map/ppermute | solution.py:22
  53.8 0.2 fusion.23
  54.0 1.9 %collective-permute-start.11 = (f32[2,2,1,256]{3,2,1,0:T(1,128)S(1)}, f32[2,2,1,256]{3,2,1,0:T(1,128)S(1)}, u32[]{:S(2)}, u32[]{:S(2)}) collective-permute-start(f32[2,2,1,256]{3,2,1,0:T(1,128)S(1)} %get-tuple-element.30), channel_id=1, source_target_pairs={{0,1},{1,2},{2,3},{4,5},{5,6},{6,7},{8,9},{9,10},{10,11},{12,13},{... | collective-permute-start | bytes 12296 | tf_op jit(solution)/shard_map/ppermute | solution.py:21
  55.9 1.3 %collective-permute-start.10 = (f32[2,2,1,256]{3,2,1,0:T(1,128)S(1)}, f32[2,2,1,256]{3,2,1,0:T(1,128)S(1)}, u32[]{:S(2)}, u32[]{:S(2)}) collective-permute-start(f32[2,2,1,256]{3,2,1,0:T(1,128)S(1)} %get-tuple-element.29), channel_id=1, source_target_pairs={{1,0},{2,1},{3,2},{5,4},{6,5},{7,6},{9,8},{10,9},{11,10},{13,12},{... | collective-permute-start | bytes 12296 | tf_op jit(solution)/shard_map/ppermute | solution.py:22
  57.2 0.1 fusion.70
  57.4 4.1 %collective-permute-done.10 = f32[2,2,1,256]{3,2,1,0:T(1,128)S(1)} collective-permute-done((f32[2,2,1,256]{3,2,1,0:T(1,128)S(1)}, f32[2,2,1,256]{3,2,1,0:T(1,128)S(1)}, u32[]{:S(2)}, u32[]{:S(2)}) %collective-permute-start.10) | collective-permute-done | bytes 4128 | tf_op jit(solution)/shard_map/ppermute | solution.py:22
  61.4 0.2 fusion.15
  61.6 1.9 %collective-permute-start.13 = (f32[2,2,1,256]{3,2,1,0:T(1,128)S(1)}, f32[2,2,1,256]{3,2,1,0:T(1,128)S(1)}, u32[]{:S(2)}, u32[]{:S(2)}) collective-permute-start(f32[2,2,1,256]{3,2,1,0:T(1,128)S(1)} %get-tuple-element.26), channel_id=1, source_target_pairs={{0,1},{1,2},{2,3},{4,5},{5,6},{6,7},{8,9},{9,10},{10,11},{12,13},{... | collective-permute-start | bytes 12296 | tf_op jit(solution)/shard_map/ppermute | solution.py:21
  63.6 1.3 %collective-permute-start.12 = (f32[2,2,1,256]{3,2,1,0:T(1,128)S(1)}, f32[2,2,1,256]{3,2,1,0:T(1,128)S(1)}, u32[]{:S(2)}, u32[]{:S(2)}) collective-permute-start(f32[2,2,1,256]{3,2,1,0:T(1,128)S(1)} %get-tuple-element.25), channel_id=1, source_target_pairs={{1,0},{2,1},{3,2},{5,4},{6,5},{7,6},{9,8},{10,9},{11,10},{13,12},{... | collective-permute-start | bytes 12296 | tf_op jit(solution)/shard_map/ppermute | solution.py:22
  64.9 0.1 fusion.68
  65.0 4.1 %collective-permute-done.12 = f32[2,2,1,256]{3,2,1,0:T(1,128)S(1)} collective-permute-done((f32[2,2,1,256]{3,2,1,0:T(1,128)S(1)}, f32[2,2,1,256]{3,2,1,0:T(1,128)S(1)}, u32[]{:S(2)}, u32[]{:S(2)}) %collective-permute-start.12) | collective-permute-done | bytes 4128 | tf_op jit(solution)/shard_map/ppermute | solution.py:22
  69.1 0.2 fusion.7
  69.3 0.5 copy.17
  69.8 14.7 %all_to_all.15 = f32[5,2,64,256]{3,1,0,2:T(2,128)S(1)} all-to-all(f32[5,2,64,256]{3,1,0,2:T(2,128)S(1)} %copy.17), channel_id=1, replica_groups=mesh['sec'=8,'tile'=4] {'sec'}, dimensions={2} | all-to-all | bytes 1310720 | tf_op jit(solution)/shard_map/all_to_all | solution.py:80
  84.8 0.9 copy-done.1
  85.9 0.1 multiply_add_fusion.6
  86.1 0.1 multiply_add_fusion.5
  86.4 0.1 multiply_add_fusion.4
  87.3 0.8 multiply_add_fusion
  (64 shorter events, 1.7 us)
Async XLA Ops:
  1.0 16.0 %collective-permute-start.1 = (f32[2,2,1,256]{3,2,1,0:T(1,128)S(1)}, f32[2,2,1,256]{3,2,1,0:T(1,128)S(1)}, u32[]{:S(2)}, u32[]{:S(2)}) collective-permute-start(f32[2,2,1,256]{3,2,1,0:T(1,128)S(1)} %get-tuple-element.50), channel_id=1, source_target_pairs={{0,1},{1,2},{2,3},{4,5},{5,6},{6,7},{8,9},{9,10},{10,11},{12,13},{... | collective-permute-start | bytes 12296 | tf_op jit(solution)/shard_map/ppermute | solution.py:21
  5.9 1.6 %copy-start.5 = (s32[1,1,256,1]{2,3,1,0:T(1,128)S(1)}, s32[1,1,256,1]{2,3,1,0:T(1,128)}, u32[]{:S(2)}) copy-start(s32[1,1,256,1]{2,3,1,0:T(1,128)} %param.10) | copy-start | bytes 3076
  5.9 1.6 %copy-start.6 = (s32[1,1,256]{2,1,0:T(1,128)S(1)}, s32[1,1,256]{2,1,0:T(1,128)}, u32[]{:S(2)}) copy-start(s32[1,1,256]{2,1,0:T(1,128)} %param.11) | copy-start | bytes 3076
  6.0 1.6 %copy-start.3 = (f32[1,1,256,128]{3,2,1,0:T(8,128)S(1)}, f32[1,1,256,128]{3,2,1,0:T(8,128)}, u32[]{:S(2)}) copy-start(f32[1,1,256,128]{3,2,1,0:T(8,128)} %param.13) | copy-start | bytes 393220
  6.0 1.6 %copy-start.4 = (f32[1,1,256,2,128]{4,3,2,1,0:T(2,128)S(1)}, f32[1,1,256,2,128]{4,3,2,1,0:T(2,128)}, u32[]{:S(2)}) copy-start(f32[1,1,256,2,128]{4,3,2,1,0:T(2,128)} %param.12) | copy-start | bytes 786436
  6.0 11.0 %collective-permute-start = (f32[2,2,1,256]{3,2,1,0:T(1,128)S(1)}, f32[2,2,1,256]{3,2,1,0:T(1,128)S(1)}, u32[]{:S(2)}, u32[]{:S(2)}) collective-permute-start(f32[2,2,1,256]{3,2,1,0:T(1,128)S(1)} %get-tuple-element.49), channel_id=1, source_target_pairs={{1,0},{2,1},{3,2},{5,4},{6,5},{7,6},{9,8},{10,9},{11,10},{13,12},{... | collective-permute-start | bytes 12296 | tf_op jit(solution)/shard_map/ppermute | solution.py:22
  16.7 1.0 %copy-start = (f32[2,2,64,256]{3,2,1,0:T(8,128)S(1)}, f32[2,2,64,256]{3,2,1,0:T(8,128)}, u32[]{:S(2)}) copy-start(f32[2,2,64,256]{3,2,1,0:T(8,128)} %param.7) | copy-start | bytes 786436
  16.7 1.0 %copy-start.2 = (f32[2,64,256]{2,1,0:T(8,128)S(1)}, f32[2,64,256]{2,1,0:T(8,128)}, u32[]{:S(2)}) copy-start(f32[2,64,256]{2,1,0:T(8,128)} %param.8) | copy-start | bytes 393220
  17.8 6.0 %collective-permute-start.3 = (f32[2,2,1,256]{3,2,1,0:T(1,128)S(1)}, f32[2,2,1,256]{3,2,1,0:T(1,128)S(1)}, u32[]{:S(2)}, u32[]{:S(2)}) collective-permute-start(f32[2,2,1,256]{3,2,1,0:T(1,128)S(1)} %get-tuple-element.46), channel_id=1, source_target_pairs={{0,1},{1,2},{2,3},{4,5},{5,6},{6,7},{8,9},{9,10},{10,11},{12,13},{... | collective-permute-start | bytes 12296 | tf_op jit(solution)/shard_map/ppermute | solution.py:21
  22.4 5.5 %collective-permute-start.2 = (f32[2,2,1,256]{3,2,1,0:T(1,128)S(1)}, f32[2,2,1,256]{3,2,1,0:T(1,128)S(1)}, u32[]{:S(2)}, u32[]{:S(2)}) collective-permute-start(f32[2,2,1,256]{3,2,1,0:T(1,128)S(1)} %get-tuple-element.45), channel_id=1, source_target_pairs={{1,0},{2,1},{3,2},{5,4},{6,5},{7,6},{9,8},{10,9},{11,10},{13,12},{... | collective-permute-start | bytes 12296 | tf_op jit(solution)/shard_map/ppermute | solution.py:22
  28.1 4.9 %collective-permute-start.5 = (f32[2,2,1,256]{3,2,1,0:T(1,128)S(1)}, f32[2,2,1,256]{3,2,1,0:T(1,128)S(1)}, u32[]{:S(2)}, u32[]{:S(2)}) collective-permute-start(f32[2,2,1,256]{3,2,1,0:T(1,128)S(1)} %get-tuple-element.42), channel_id=1, source_target_pairs={{0,1},{1,2},{2,3},{4,5},{5,6},{6,7},{8,9},{9,10},{10,11},{12,13},{... | collective-permute-start | bytes 12296 | tf_op jit(solution)/shard_map/ppermute | solution.py:21
  31.5 5.5 %collective-permute-start.4 = (f32[2,2,1,256]{3,2,1,0:T(1,128)S(1)}, f32[2,2,1,256]{3,2,1,0:T(1,128)S(1)}, u32[]{:S(2)}, u32[]{:S(2)}) collective-permute-start(f32[2,2,1,256]{3,2,1,0:T(1,128)S(1)} %get-tuple-element.41), channel_id=1, source_target_pairs={{1,0},{2,1},{3,2},{5,4},{6,5},{7,6},{9,8},{10,9},{11,10},{13,12},{... | collective-permute-start | bytes 12296 | tf_op jit(solution)/shard_map/ppermute | solution.py:22
  37.2 4.9 %collective-permute-start.7 = (f32[2,2,1,256]{3,2,1,0:T(1,128)S(1)}, f32[2,2,1,256]{3,2,1,0:T(1,128)S(1)}, u32[]{:S(2)}, u32[]{:S(2)}) collective-permute-start(f32[2,2,1,256]{3,2,1,0:T(1,128)S(1)} %get-tuple-element.38), channel_id=1, source_target_pairs={{0,1},{1,2},{2,3},{4,5},{5,6},{6,7},{8,9},{9,10},{10,11},{12,13},{... | collective-permute-start | bytes 12296 | tf_op jit(solution)/shard_map/ppermute | solution.py:21
  40.7 5.5 %collective-permute-start.6 = (f32[2,2,1,256]{3,2,1,0:T(1,128)S(1)}, f32[2,2,1,256]{3,2,1,0:T(1,128)S(1)}, u32[]{:S(2)}, u32[]{:S(2)}) collective-permute-start(f32[2,2,1,256]{3,2,1,0:T(1,128)S(1)} %get-tuple-element.37), channel_id=1, source_target_pairs={{1,0},{2,1},{3,2},{5,4},{6,5},{7,6},{9,8},{10,9},{11,10},{13,12},{... | collective-permute-start | bytes 12296 | tf_op jit(solution)/shard_map/ppermute | solution.py:22
  46.4 3.4 %collective-permute-start.9 = (f32[2,2,1,256]{3,2,1,0:T(1,128)S(1)}, f32[2,2,1,256]{3,2,1,0:T(1,128)S(1)}, u32[]{:S(2)}, u32[]{:S(2)}) collective-permute-start(f32[2,2,1,256]{3,2,1,0:T(1,128)S(1)} %get-tuple-element.34), channel_id=1, source_target_pairs={{0,1},{1,2},{2,3},{4,5},{5,6},{6,7},{8,9},{9,10},{10,11},{12,13},{... | collective-permute-start | bytes 12296 | tf_op jit(solution)/shard_map/ppermute | solution.py:21
  48.3 5.5 %collective-permute-start.8 = (f32[2,2,1,256]{3,2,1,0:T(1,128)S(1)}, f32[2,2,1,256]{3,2,1,0:T(1,128)S(1)}, u32[]{:S(2)}, u32[]{:S(2)}) collective-permute-start(f32[2,2,1,256]{3,2,1,0:T(1,128)S(1)} %get-tuple-element.33), channel_id=1, source_target_pairs={{1,0},{2,1},{3,2},{5,4},{6,5},{7,6},{9,8},{10,9},{11,10},{13,12},{... | collective-permute-start | bytes 12296 | tf_op jit(solution)/shard_map/ppermute | solution.py:22
  54.0 3.4 %collective-permute-start.11 = (f32[2,2,1,256]{3,2,1,0:T(1,128)S(1)}, f32[2,2,1,256]{3,2,1,0:T(1,128)S(1)}, u32[]{:S(2)}, u32[]{:S(2)}) collective-permute-start(f32[2,2,1,256]{3,2,1,0:T(1,128)S(1)} %get-tuple-element.30), channel_id=1, source_target_pairs={{0,1},{1,2},{2,3},{4,5},{5,6},{6,7},{8,9},{9,10},{10,11},{12,13},{... | collective-permute-start | bytes 12296 | tf_op jit(solution)/shard_map/ppermute | solution.py:21
  55.9 5.5 %collective-permute-start.10 = (f32[2,2,1,256]{3,2,1,0:T(1,128)S(1)}, f32[2,2,1,256]{3,2,1,0:T(1,128)S(1)}, u32[]{:S(2)}, u32[]{:S(2)}) collective-permute-start(f32[2,2,1,256]{3,2,1,0:T(1,128)S(1)} %get-tuple-element.29), channel_id=1, source_target_pairs={{1,0},{2,1},{3,2},{5,4},{6,5},{7,6},{9,8},{10,9},{11,10},{13,12},{... | collective-permute-start | bytes 12296 | tf_op jit(solution)/shard_map/ppermute | solution.py:22
  61.6 3.4 %collective-permute-start.13 = (f32[2,2,1,256]{3,2,1,0:T(1,128)S(1)}, f32[2,2,1,256]{3,2,1,0:T(1,128)S(1)}, u32[]{:S(2)}, u32[]{:S(2)}) collective-permute-start(f32[2,2,1,256]{3,2,1,0:T(1,128)S(1)} %get-tuple-element.26), channel_id=1, source_target_pairs={{0,1},{1,2},{2,3},{4,5},{5,6},{6,7},{8,9},{9,10},{10,11},{12,13},{... | collective-permute-start | bytes 12296 | tf_op jit(solution)/shard_map/ppermute | solution.py:21
  63.6 5.5 %collective-permute-start.12 = (f32[2,2,1,256]{3,2,1,0:T(1,128)S(1)}, f32[2,2,1,256]{3,2,1,0:T(1,128)S(1)}, u32[]{:S(2)}, u32[]{:S(2)}) collective-permute-start(f32[2,2,1,256]{3,2,1,0:T(1,128)S(1)} %get-tuple-element.25), channel_id=1, source_target_pairs={{1,0},{2,1},{3,2},{5,4},{6,5},{7,6},{9,8},{10,9},{11,10},{13,12},{... | collective-permute-start | bytes 12296 | tf_op jit(solution)/shard_map/ppermute | solution.py:22
  84.8 0.9 %copy-start.1 = (f32[16,8,256]{2,1,0:T(8,128)S(1)}, f32[16,8,256]{2,1,0:T(8,128)}, u32[]{:S(2)}) copy-start(f32[16,8,256]{2,1,0:T(8,128)} %param.9) | copy-start | bytes 393220
where the time goes:
time: 88.8 us; the launch traced here: 88.1 us
  starting transfers between devices  31.4 us (35%)
  waiting for transfers between devices  24.3 us (27%)
  blocking collectives  14.7 us (17%)
  other arithmetic  12.8 us (14%)
  local copies, waits for them, and re-layouts  4.16 us (5%)
    ppermute x7, waiting for transfers between devices, padded(): after = lax.ppermute(leading, axis, down)  24.3 us
    ppermute x7, starting transfers between devices, padded(): before = lax.ppermute(last, axis, up)  22.2 us
    all_to_all x1, blocking collectives, per_device(): lax.all_to_all(stacked, 'sec', split_axis=2, concat_axis=1, tiled=True)  14.7 us
    ppermute x7, starting transfers between devices, padded(): after = lax.ppermute(leading, axis, down)  9.18 us
    scatter-add x1, other arithmetic, spread(): jnp.zeros((layers * rows * blocks, 3, width), jnp.float32).at[target]  8.35 us
  transfers between devices with their start and end apart: 14, of which 6 were waited for; matrix products, arithmetic and copies ran while one was open for 12% of the time, Pallas kernels for 0%

commit v1 on v0

v1 whole, which is shorter than its diff:
```python
import functools

import jax
import jax.numpy as jnp
from jax import lax
from jax.experimental import pallas as pl
from jax.experimental.pallas import tpu as pltpu
from jax.sharding import PartitionSpec as P

ISTEPS = 8
ZSTEPS = 8


STEP_PLANE = 0.12
STEP_CROSS = 0.15

HALO = -(-(ISTEPS - 1) // 8) * 8

VMEM = pl.BlockSpec(memory_space=pltpu.VMEM)


def spread_kernel(layers, inner_rows, blocks, dest_ref, pos_ref, flow_ref, conf_ref, out_ref):
    groups = out_ref.shape[0]
    count, width = conf_ref.shape
    place = pos_ref[...]
    layer = place // (inner_rows * blocks)
    inner_row = place // blocks % inner_rows
    column_block = place % blocks
    slot = (dest_ref[...] * layers + layer) * inner_rows + inner_row
    slots = groups * layers * inner_rows
    conf = conf_ref[...]
    terms = [flow_ref[pl.ds(c, count, stride=2), :] * conf for c in range(2)] + [conf]
    rest = jnp.concatenate(terms, axis=1)
    parts = []
    for _ in range(3):
        parts.append(rest.astype(jnp.bfloat16))
        rest = rest - parts[-1].astype(jnp.float32)
    numbers = lax.broadcasted_iota(jnp.int32, (slots, count), 0)
    for b in range(blocks):
        key = jnp.where(column_block == b, slot, -1)
        hit = jnp.where(numbers == key, 1.0, 0.0).astype(jnp.bfloat16)
        total = sum(jnp.dot(hit, part, preferred_element_type=jnp.float32) for part in reversed(parts))
        for o in range(groups):
            for l in range(layers):
                start = (o * layers + l) * inner_rows
                for c in range(3):
                    out_ref[o, c, l, :, b * width : (b + 1) * width] = total[
                        start : start + inner_rows, c * width : (c + 1) * width
                    ]


def shifted(blocks, lane, width):
    ahead = [pltpu.roll(x, width - 1, 1) for x in blocks]
    behind = [pltpu.roll(x, 1, 1) for x in blocks]
    zero = jnp.zeros_like(blocks[0])
    right = [jnp.where(lane == width - 1, after, own) for own, after in zip(ahead, ahead[1:] + [zero])]
    left = [jnp.where(lane == 0, before, own) for own, before in zip(behind, [zero] + behind[:-1])]
    return left, right


def plane_kernel(force_ref, stiff_ref, before_ref, after_ref, forces_ref, out_ref):
    _, layers, rows, columns = force_ref.shape
    out_ref[:, 2:] = forces_ref[...]
    groups = out_ref.shape[0]
    inner_rows = rows // groups
    width = 128
    total = rows + 2 * HALO
    lane = lax.broadcasted_iota(jnp.int32, (total, width), 1)
    spans = [slice(i * width, (i + 1) * width) for i in range(columns // width)]
    for l in range(layers):
        spring, keep = [], []
        for span in spans:
            k = STEP_PLANE * jnp.concatenate(
                [before_ref[2, l, :, span], stiff_ref[l, :, span], after_ref[2, l, :, span]], axis=0
            )
            spring.append(k)
            keep.append(1.0 - 4.0 * k)
        for c in range(2):
            push = [
                STEP_PLANE
                * jnp.concatenate(
                    [before_ref[c, l, :, span], force_ref[c, l, :, span], after_ref[c, l, :, span]], axis=0
                )
                for span in spans
            ]
            field = push
            for step in range(1, ISTEPS):
                left, right = shifted(field, lane, width)
                field = [
                    k * (pltpu.roll(x, 1, 0) + pltpu.roll(x, total - 1, 0) + a + b) + (g * x + f)
                    for x, a, b, k, g, f in zip(field, left, right, spring, keep, push)
                ]
            for span, x in zip(spans, field):
                for o in range(groups):
                    start = HALO + o * inner_rows
                    out_ref[o, c, l, :, span] = x[start : start + inner_rows]


def cross_kernel(moved_ref, stiff_ref, out_ref):
    groups, _, layers, inner_rows, columns = moved_ref.shape
    sections = groups * layers
    width = 128
    zero = jnp.zeros((1, inner_rows, width), jnp.float32)
    for i in range(columns // width):
        span = slice(i * width, (i + 1) * width)

        def channel(c):
            return moved_ref[:, c, :, :, span].reshape(sections, inner_rows, width)

        spring = STEP_CROSS * stiff_ref[:, :, span]
        weight = STEP_CROSS * channel(4)
        for c in range(2):
            pull = STEP_CROSS * channel(2 + c)
            field = channel(c)
            for step in range(ZSTEPS):
                rise = field - jnp.concatenate([zero, field[:-1]], axis=0)
                rise_above = jnp.concatenate([rise[1:], -field[-1:]], axis=0)
                stretch = pull - weight * rise
                stretch_above = jnp.concatenate([stretch[1:], zero], axis=0)
                field = field + (spring * (rise_above - rise) + (stretch - stretch_above))
            out_ref[c, :, :, span] = field


def per_device(
    in_plane_force, stiffness, stiffness_z, patch_dest, patch_pos, patch_flow, patch_conf
):
    groups = lax.axis_size("sec")
    tiles = lax.axis_size("tile")
    layers, rows, columns = stiffness.shape
    inner_rows = rows // groups
    width = patch_flow.shape[-1]
    blocks = columns // width
    count = patch_pos.shape[2]
    up = [(i, i + 1) for i in range(tiles - 1)]
    down = [(j, i) for i, j in up]

    def edge(start):
        return jnp.concatenate(
            [in_plane_force[:, :, start : start + HALO], stiffness[None, :, start : start + HALO]], axis=0
        )

    before = lax.ppermute(edge(rows - HALO), "tile", up)
    after = lax.ppermute(edge(0), "tile", down)
    forces = pl.pallas_call(
        functools.partial(spread_kernel, layers, inner_rows, blocks),
        out_shape=jax.ShapeDtypeStruct((groups, 3, layers, inner_rows, columns), jnp.float32),
        in_specs=[VMEM] * 4,
        out_specs=VMEM,
        cost_estimate=pl.CostEstimate(flops=6 * 256 * 256 * 384, bytes_accessed=800000, transcendentals=0),
        name="spread_patches",
    )(
        patch_dest.reshape(1, count),
        patch_pos.reshape(1, count),
        patch_flow.reshape(count * 2, width),
        patch_conf.reshape(count, width),
    )
    mixed = pl.pallas_call(
        plane_kernel,
        out_shape=jax.ShapeDtypeStruct((groups, 5, layers, inner_rows, columns), jnp.float32),
        in_specs=[VMEM] * 5,
        out_specs=VMEM,
        cost_estimate=pl.CostEstimate(flops=10000000, bytes_accessed=800000, transcendentals=0),
        name="plane_steps",
    )(in_plane_force, stiffness, before, after, forces)
    moved = lax.all_to_all(mixed, "sec", split_axis=0, concat_axis=0, tiled=True)
    return pl.pallas_call(
        cross_kernel,
        out_shape=jax.ShapeDtypeStruct((2, groups * layers, inner_rows, columns), jnp.float32),
        in_specs=[VMEM] * 2,
        out_specs=VMEM,
        cost_estimate=pl.CostEstimate(flops=10000000, bytes_accessed=800000, transcendentals=0),
        name="cross_steps",
    )(moved, stiffness_z)


def solution(mesh):
    placed = (
        P(None, "sec", "tile", None),
        P("sec", "tile", None),
        P(None, ("tile", "sec"), None),
        P("sec", "tile", None, None),
        P("sec", "tile", None),
        P("sec", "tile", None, None, None),
        P("sec", "tile", None, None),
    )
    return jax.shard_map(
        per_device,
        mesh=mesh,
        in_specs=placed,
        out_specs=P(None, None, ("tile", "sec"), None),
        check_vma=False,
    )
```

time: 88.8 us -> 35.9 us (0.40)
  starting transfers between devices: 31.4 us -> 6.22 us
  waiting for transfers between devices: 24.3 us -> 2.53 us
  other arithmetic: 12.8 us -> 0.01 us
  Pallas kernels: 0 us -> 9.19 us
  local copies, waits for them, and re-layouts: 4.16 us -> 2.14 us
    ppermute x14 -> x2, starting transfers between devices: 31.4 us -> 6.22 us  [the longest x1 4.93 us: per_device(): before = lax.ppermute(edge(rows - HALO), 'tile', up)]
    ppermute x14 -> x2, waiting for transfers between devices: 24.3 us -> 2.53 us  [the longest x1 2.53 us: per_device(): after = lax.ppermute(edge(0), 'tile', down)]
    pallas_call x0 -> x3, Pallas kernels: none -> 9.19 us  [the longest x1 4.47 us: per_device(): pl.pallas_call(plane_kernel, out_shape=jax.ShapeDtypeStruct((groups, 5, l...]
    scatter-add x1 -> x0, other arithmetic: 8.35 us -> none  [spread(): jnp.zeros((layers * rows * blocks, 3, width), jnp.float32).at[target]]
    add x15 -> x0, other arithmetic: 2.57 us -> none  [the longest x8 1.46 us: cross_steps(): field + STEP_CROSS * (stiffness_z[None] * (above + below - 2.0 * field) +...]
    mul x2 -> x0, other arithmetic: 1.11 us -> none  [the longest x1 0.97 us: per_device(): field = STEP_PLANE * in_plane_force]
    unnamed x14 -> x4, local copies, waits for them, and re-layouts: 1.52 us -> 0.62 us
  transfers between devices with their start and end apart: 14 -> 2, of which waited for: 6 -> 1; matrix products, arithmetic and copies ran while one was open for 12% -> 0% of each run, Pallas kernels for 0% -> 6%
where the time goes in v1:
time: 35.9 us; the launch traced here: 35.5 us
  blocking collectives  15.3 us (43%)
  Pallas kernels  9.19 us (26%)
  starting transfers between devices  6.22 us (17%)
  waiting for transfers between devices  2.53 us (7%)
  local copies, waits for them, and re-layouts  2.14 us (6%)
    all_to_all x1, blocking collectives, per_device(): lax.all_to_all(mixed, 'sec', split_axis=0, concat_axis=0, tiled=True)  15.3 us
    ppermute x1, starting transfers between devices, per_device(): before = lax.ppermute(edge(rows - HALO), 'tile', up)  4.93 us
    pallas_call x1, Pallas kernels, per_device(): pl.pallas_call(plane_kernel, out_shape=jax.ShapeDtypeStruct((groups, 5, l...  4.47 us
    pallas_call x1, Pallas kernels, per_device(): pl.pallas_call(cross_kernel, out_shape=jax.ShapeDtypeStruct((2, groups *...  2.57 us
    ppermute x1, waiting for transfers between devices, per_device(): after = lax.ppermute(edge(0), 'tile', down)  2.53 us
    pallas_call x1, Pallas kernels, per_device(): pl.pallas_call(functools.partial(spread_kernel, layers, inner_rows, block...  2.15 us
    ppermute x1, starting transfers between devices, per_device(): after = lax.ppermute(edge(0), 'tile', down)  1.29 us
    slice x1, local copies, waits for them, and re-layouts, edge(): in_plane_force[:, :, start:start + HALO]  0.78 us
  transfers between devices with their start and end apart: 2, of which 1 were waited for; matrix products, arithmetic and copies ran while one was open for 0% of the time, Pallas kernels for 6%

profile of v1, /device:TPU:0, one launch (start us, length us, event | category | flops | bytes accessed | tf_op | source)
XLA Modules:
  0.0 35.5 jit_solution(7530025625127736067)
XLA Ops:
  0.0 0.7 %slice_bitcast_fusion = (f32[1,2,8,256]{3,2,1,0:T(8,128)S(1)}, f32[1,2,8,256]{3,2,1,0:T(8,128)S(1)}) fusion(f32[2,64,256]{2,1,0:T(8,128)} %stiff_ref.2), kind=kLoop, calls=%fused_computation.2 | loop fusion | bytes 65536 | tf_op jit(solution)/shard_map/broadcast_in_dim | solution.py:139
  0.7 0.8 %fusion = (f32[2,2,8,256]{3,2,1,0:T(8,128)S(1)}, f32[2,2,8,256]{3,2,1,0:T(8,128)S(1)}) fusion(f32[2,2,64,256]{3,2,1,0:T(8,128)} %force_ref.1), kind=kLoop, calls=%fused_computation.4 | loop fusion | bytes 131072 | tf_op jit(solution)/shard_map/slice | solution.py:139
  1.5 4.9 %collective-permute-start = (f32[3,2,8,256]{3,2,1,0:T(8,128)S(1)}, f32[3,2,8,256]{3,2,1,0:T(8,128)S(1)}, u32[]{:S(2)}, u32[]{:S(2)}) collective-permute-start(f32[3,2,8,256]{3,2,1,0:T(8,128)S(1)} %pad_maximum_fusion), channel_id=1, source_target_pairs={{0,1},{1,2},{2,3},{4,5},{5,6},{6,7},{8,9},{9,10},{10,11},{12,13},{... | collective-permute-start | bytes 147464 | tf_op jit(solution)/shard_map/ppermute | solution.py:142
  6.5 1.3 %collective-permute-start.1 = (f32[3,2,8,256]{3,2,1,0:T(8,128)S(1)}, f32[3,2,8,256]{3,2,1,0:T(8,128)S(1)}, u32[]{:S(2)}, u32[]{:S(2)}) collective-permute-start(f32[3,2,8,256]{3,2,1,0:T(8,128)S(1)} %pad_maximum_fusion.1), channel_id=1, source_target_pairs={{1,0},{2,1},{3,2},{5,4},{6,5},{7,6},{9,8},{10,9},{11,10},{13,12},{... | collective-permute-start | bytes 147464 | tf_op jit(solution)/shard_map/ppermute | solution.py:143
  7.8 2.1 %spread_patches.1.forces_ref = f32[8,3,2,8,256]{4,3,2,1,0:T(8,128)} custom-call(s32[1,256]{1,0:T(1,128)} %bitcast.10, s32[1,256]{1,0:T(1,128)} %bitcast.11, f32[512,128]{1,0:T(8,128)} %bitcast.8, f32[256,128]{1,0:T(8,128)} %bitcast.9), custom_call_target="tpu_custom_call" | custom-call | flops 150994944 | bytes 800000 | tf_op jit(solution)/shard_map/spread_patches/pallas_call | solution.py:144
  9.9 0.0 collective-permute-done.before_ref
  9.9 0.0 copy-start
  9.9 2.5 %collective-permute-done.1.after_ref = f32[3,2,8,256]{3,2,1,0:T(8,128)S(1)} collective-permute-done((f32[3,2,8,256]{3,2,1,0:T(8,128)S(1)}, f32[3,2,8,256]{3,2,1,0:T(8,128)S(1)}, u32[]{:S(2)}, u32[]{:S(2)}) %collective-permute-start.1) | collective-permute-done | bytes 49184 | tf_op jit(solution)/shard_map/ppermute | solution.py:143
  12.5 0.0 copy-done
  12.5 0.0 copy-start.1
  12.5 0.6 %copy-done.1 = f32[3,2,8,256]{3,2,1,0:T(8,128)} copy-done((f32[3,2,8,256]{3,2,1,0:T(8,128)}, f32[3,2,8,256]{3,2,1,0:T(8,128)S(1)}, u32[]{:S(2)}) %copy-start.1) | copy-done | bytes 49176
  13.1 4.5 %plane_steps.1 = f32[8,5,2,8,256]{4,3,2,1,0:T(8,128)} custom-call(f32[2,2,64,256]{3,2,1,0:T(8,128)} %force_ref.1, f32[2,64,256]{2,1,0:T(8,128)} %stiff_ref.2, f32[3,2,8,256]{3,2,1,0:T(8,128)} %copy-done, f32[3,2,8,256]{3,2,1,0:T(8,128)} %copy-done.1, f32[8,3,2,8,256]{4,3,2,1,0:T(8,128)} %spread_patches.1.forces_ref), custom_call_target="tpu_custom_call" | custom-call | flops 10000000 | bytes 800000 | tf_op jit(solution)/shard_map/plane_steps/pallas_call | solution.py:157
  17.6 15.3 %all_to_all.5.moved_ref = f32[8,5,2,8,256]{4,3,2,1,0:T(8,128)} all-to-all(f32[8,5,2,8,256]{4,3,2,1,0:T(8,128)} %plane_steps.1), channel_id=1, replica_groups=mesh['sec'=8,'tile'=4] {'sec'}, dimensions={0} | all-to-all | bytes 1310720 | tf_op jit(solution)/shard_map/all_to_all | solution.py:165
  32.9 2.6 %cross_steps.1 = f32[2,16,8,256]{3,2,1,0:T(8,128)} custom-call(f32[8,5,2,8,256]{4,3,2,1,0:T(8,128)} %all_to_all.5.moved_ref, f32[16,8,256]{2,1,0:T(8,128)} %stiff_ref.3), custom_call_target="tpu_custom_call" | custom-call | flops 10000000 | bytes 800000 | tf_op jit(solution)/shard_map/cross_steps/pallas_call | solution.py:166
  (2 shorter events, 0.0 us)
Async XLA Ops:
  1.5 8.4 %collective-permute-start = (f32[3,2,8,256]{3,2,1,0:T(8,128)S(1)}, f32[3,2,8,256]{3,2,1,0:T(8,128)S(1)}, u32[]{:S(2)}, u32[]{:S(2)}) collective-permute-start(f32[3,2,8,256]{3,2,1,0:T(8,128)S(1)} %pad_maximum_fusion), channel_id=1, source_target_pairs={{0,1},{1,2},{2,3},{4,5},{5,6},{6,7},{8,9},{9,10},{10,11},{12,13},{... | collective-permute-start | bytes 147464 | tf_op jit(solution)/shard_map/ppermute | solution.py:142
  6.5 6.0 %collective-permute-start.1 = (f32[3,2,8,256]{3,2,1,0:T(8,128)S(1)}, f32[3,2,8,256]{3,2,1,0:T(8,128)S(1)}, u32[]{:S(2)}, u32[]{:S(2)}) collective-permute-start(f32[3,2,8,256]{3,2,1,0:T(8,128)S(1)} %pad_maximum_fusion.1), channel_id=1, source_target_pairs={{1,0},{2,1},{3,2},{5,4},{6,5},{7,6},{9,8},{10,9},{11,10},{13,12},{... | collective-permute-start | bytes 147464 | tf_op jit(solution)/shard_map/ppermute | solution.py:143
  9.9 2.5 %copy-start = (f32[3,2,8,256]{3,2,1,0:T(8,128)}, f32[3,2,8,256]{3,2,1,0:T(8,128)S(1)}, u32[]{:S(2)}) copy-start(f32[3,2,8,256]{3,2,1,0:T(8,128)S(1)} %collective-permute-done.before_ref) | copy-start | bytes 147460
  12.5 0.6 %copy-start.1 = (f32[3,2,8,256]{3,2,1,0:T(8,128)}, f32[3,2,8,256]{3,2,1,0:T(8,128)S(1)}, u32[]{:S(2)}) copy-start(f32[3,2,8,256]{3,2,1,0:T(8,128)S(1)} %collective-permute-done.1.after_ref) | copy-start | bytes 147460

commit v2 on v1

--- a/solution.py
+++ b/solution.py
@@ -58,9 +58,8 @@
     return left, right
 
 
-def plane_kernel(force_ref, stiff_ref, before_ref, after_ref, forces_ref, out_ref):
+def plane_kernel(force_ref, stiff_ref, before_ref, after_ref, out_ref):
     _, layers, rows, columns = force_ref.shape
-    out_ref[:, 2:] = forces_ref[...]
     groups = out_ref.shape[0]
     inner_rows = rows // groups
     width = 128
@@ -96,7 +95,7 @@
                     out_ref[o, c, l, :, span] = x[start : start + inner_rows]
 
 
-def cross_kernel(moved_ref, stiff_ref, out_ref):
+def cross_kernel(moved_ref, forces_ref, stiff_ref, out_ref):
     groups, _, layers, inner_rows, columns = moved_ref.shape
     sections = groups * layers
     width = 128
@@ -104,14 +103,14 @@
     for i in range(columns // width):
         span = slice(i * width, (i + 1) * width)
 
-        def channel(c):
-            return moved_ref[:, c, :, :, span].reshape(sections, inner_rows, width)
+        def channel(ref, c):
+            return ref[:, c, :, :, span].reshape(sections, inner_rows, width)
 
         spring = STEP_CROSS * stiff_ref[:, :, span]
-        weight = STEP_CROSS * channel(4)
+        weight = STEP_CROSS * channel(forces_ref, 2)
         for c in range(2):
-            pull = STEP_CROSS * channel(2 + c)
-            field = channel(c)
+            pull = STEP_CROSS * channel(forces_ref, c)
+            field = channel(moved_ref, c)
             for step in range(ZSTEPS):
                 rise = field - jnp.concatenate([zero, field[:-1]], axis=0)
                 rise_above = jnp.concatenate([rise[1:], -field[-1:]], axis=0)
@@ -154,23 +153,24 @@
         patch_flow.reshape(count * 2, width),
         patch_conf.reshape(count, width),
     )
-    mixed = pl.pallas_call(
+    forces = lax.all_to_all(forces, "sec", split_axis=0, concat_axis=0, tiled=True)
+    planar = pl.pallas_call(
         plane_kernel,
-        out_shape=jax.ShapeDtypeStruct((groups, 5, layers, inner_rows, columns), jnp.float32),
-        in_specs=[VMEM] * 5,
+        out_shape=jax.ShapeDtypeStruct((groups, 2, layers, inner_rows, columns), jnp.float32),
+        in_specs=[VMEM] * 4,
         out_specs=VMEM,
         cost_estimate=pl.CostEstimate(flops=10000000, bytes_accessed=800000, transcendentals=0),
         name="plane_steps",
-    )(in_plane_force, stiffness, before, after, forces)
-    moved = lax.all_to_all(mixed, "sec", split_axis=0, concat_axis=0, tiled=True)
+    )(in_plane_force, stiffness, before, after)
+    moved = lax.all_to_all(planar, "sec", split_axis=0, concat_axis=0, tiled=True)
     return pl.pallas_call(
         cross_kernel,
         out_shape=jax.ShapeDtypeStruct((2, groups * layers, inner_rows, columns), jnp.float32),
-        in_specs=[VMEM] * 2,
+        in_specs=[VMEM] * 3,
         out_specs=VMEM,
         cost_estimate=pl.CostEstimate(flops=10000000, bytes_accessed=800000, transcendentals=0),
         name="cross_steps",
-    )(moved, stiffness_z)
+    )(moved, forces, stiffness_z)
 
 
 def solution(mesh):

time: 35.9 us -> 43.4 us (1.21)
  waiting for transfers between devices: 2.53 us -> 9.47 us
  starting transfers between devices: 6.22 us -> 9.95 us
  blocking collectives: 15.3 us -> 12.4 us
    all_to_all x0 -> x1, waiting for transfers between devices: none -> 4.79 us  [per_device(): lax.all_to_all(planar, 'sec', split_axis=0, concat_axis=0, tiled=True)]
    all_to_all x0 -> x1, starting transfers between devices: none -> 3.72 us  [per_device(): lax.all_to_all(planar, 'sec', split_axis=0, concat_axis=0, tiled=True)]
    all_to_all x1, blocking collectives: 15.3 us -> 12.4 us  [per_device(): lax.all_to_all(forces, 'sec', split_axis=0, concat_axis=0, tiled=True)]
    ppermute x1, waiting for transfers between devices: 2.53 us -> 4.26 us  [per_device(): after = lax.ppermute(edge(0), 'tile', down)]
  transfers between devices with their start and end apart: 2 -> 3, of which waited for: 1 -> 3; matrix products, arithmetic and copies ran while one was open for 0% -> 0% of each run, Pallas kernels for 6% -> 5%
where the time goes in v2:
time: 43.4 us; the launch traced here: 42.9 us
  blocking collectives  12.4 us (29%)
  starting transfers between devices  9.95 us (23%)
  waiting for transfers between devices  9.47 us (22%)
  Pallas kernels  8.87 us (20%)
  local copies, waits for them, and re-layouts  2.14 us (5%)
    all_to_all x1, blocking collectives, per_device(): lax.all_to_all(forces, 'sec', split_axis=0, concat_axis=0, tiled=True)  12.4 us
    ppermute x1, starting transfers between devices, per_device(): before = lax.ppermute(edge(rows - HALO), 'tile', up)  4.93 us
    all_to_all x1, waiting for transfers between devices, per_device(): lax.all_to_all(planar, 'sec', split_axis=0, concat_axis=0, tiled=True)  4.79 us
    ppermute x1, waiting for transfers between devices, per_device(): after = lax.ppermute(edge(0), 'tile', down)  4.26 us
    pallas_call x1, Pallas kernels, per_device(): pl.pallas_call(plane_kernel, out_shape=jax.ShapeDtypeStruct((groups, 2, l...  4.16 us
    all_to_all x1, starting transfers between devices, per_device(): lax.all_to_all(planar, 'sec', split_axis=0, concat_axis=0, tiled=True)  3.72 us
    pallas_call x1, Pallas kernels, per_device(): pl.pallas_call(cross_kernel, out_shape=jax.ShapeDtypeStruct((2, groups *...  2.57 us
    pallas_call x1, Pallas kernels, per_device(): pl.pallas_call(functools.partial(spread_kernel, layers, inner_rows, block...  2.14 us
  transfers between devices with their start and end apart: 3, of which 3 were waited for; matrix products, arithmetic and copies ran while one was open for 0% of the time, Pallas kernels for 5%

profile of v2, /device:TPU:0, one launch (start us, length us, event | category | flops | bytes accessed | tf_op | source)
XLA Modules:
  0.0 42.9 jit_solution(7884709861130301193)
XLA Ops:
  0.0 0.7 %slice_bitcast_fusion = (f32[1,2,8,256]{3,2,1,0:T(8,128)S(1)}, f32[1,2,8,256]{3,2,1,0:T(8,128)S(1)}) fusion(f32[2,64,256]{2,1,0:T(8,128)} %stiff_ref.2), kind=kLoop, calls=%fused_computation.2 | loop fusion | bytes 65536 | tf_op jit(solution)/shard_map/broadcast_in_dim | solution.py:138
  0.7 0.8 %fusion = (f32[2,2,8,256]{3,2,1,0:T(8,128)S(1)}, f32[2,2,8,256]{3,2,1,0:T(8,128)S(1)}) fusion(f32[2,2,64,256]{3,2,1,0:T(8,128)} %force_ref.1), kind=kLoop, calls=%fused_computation.4 | loop fusion | bytes 131072 | tf_op jit(solution)/shard_map/slice | solution.py:138
  1.5 4.9 %collective-permute-start = (f32[3,2,8,256]{3,2,1,0:T(8,128)S(1)}, f32[3,2,8,256]{3,2,1,0:T(8,128)S(1)}, u32[]{:S(2)}, u32[]{:S(2)}) collective-permute-start(f32[3,2,8,256]{3,2,1,0:T(8,128)S(1)} %pad_maximum_fusion), channel_id=1, source_target_pairs={{0,1},{1,2},{2,3},{4,5},{5,6},{6,7},{8,9},{9,10},{10,11},{12,13},{... | collective-permute-start | bytes 147464 | tf_op jit(solution)/shard_map/ppermute | solution.py:141
  6.5 1.3 %collective-permute-start.1 = (f32[3,2,8,256]{3,2,1,0:T(8,128)S(1)}, f32[3,2,8,256]{3,2,1,0:T(8,128)S(1)}, u32[]{:S(2)}, u32[]{:S(2)}) collective-permute-start(f32[3,2,8,256]{3,2,1,0:T(8,128)S(1)} %pad_maximum_fusion.1), channel_id=1, source_target_pairs={{1,0},{2,1},{3,2},{5,4},{6,5},{7,6},{9,8},{10,9},{11,10},{13,12},{... | collective-permute-start | bytes 147464 | tf_op jit(solution)/shard_map/ppermute | solution.py:142
  7.8 0.4 collective-permute-done.before_ref
  8.2 0.0 copy-start.1
  8.2 4.3 %collective-permute-done.1.after_ref = f32[3,2,8,256]{3,2,1,0:T(8,128)S(1)} collective-permute-done((f32[3,2,8,256]{3,2,1,0:T(8,128)S(1)}, f32[3,2,8,256]{3,2,1,0:T(8,128)S(1)}, u32[]{:S(2)}, u32[]{:S(2)}) %collective-permute-start.1) | collective-permute-done | bytes 49184 | tf_op jit(solution)/shard_map/ppermute | solution.py:142
  12.5 0.0 copy-done.1
  12.5 0.0 copy-start.2
  12.5 0.6 %copy-done.2 = f32[3,2,8,256]{3,2,1,0:T(8,128)} copy-done((f32[3,2,8,256]{3,2,1,0:T(8,128)}, f32[3,2,8,256]{3,2,1,0:T(8,128)S(1)}, u32[]{:S(2)}) %copy-start.2) | copy-done | bytes 49176
  13.1 4.2 %plane_steps.1 = f32[8,2,2,8,256]{4,3,2,1,0:T(8,128)} custom-call(f32[2,2,64,256]{3,2,1,0:T(8,128)} %force_ref.1, f32[2,64,256]{2,1,0:T(8,128)} %stiff_ref.2, f32[3,2,8,256]{3,2,1,0:T(8,128)} %copy-done.1, f32[3,2,8,256]{3,2,1,0:T(8,128)} %copy-done.2), custom_call_target="tpu_custom_call" | custom-call | flops 10000000 | bytes 800000 | tf_op jit(solution)/shard_map/plane_steps/pallas_call | solution.py:157
  17.2 3.7 %all-to-all-start = ((f32[8,2,2,8,256]{4,3,2,1,0:T(8,128)}), f32[8,2,2,8,256]{4,3,2,1,0:T(8,128)S(1)}, u32[]{:S(2)}, u32[]{:S(2)}) async-start(f32[8,2,2,8,256]{4,3,2,1,0:T(8,128)} %plane_steps.1), calls=%async_computation | async-start | bytes 524288 | tf_op jit(solution)/shard_map/all_to_all | solution.py:165
  21.0 2.1 %spread_patches.1 = f32[8,3,2,8,256]{4,3,2,1,0:T(8,128)} custom-call(s32[1,256]{1,0:T(1,128)} %bitcast.10, s32[1,256]{1,0:T(1,128)} %bitcast.11, f32[512,128]{1,0:T(8,128)} %bitcast.8, f32[256,128]{1,0:T(8,128)} %bitcast.9), custom_call_target="tpu_custom_call" | custom-call | flops 150994944 | bytes 800000 | tf_op jit(solution)/shard_map/spread_patches/pallas_call | solution.py:143
  23.1 4.8 %all-to-all-done.moved_ref = f32[8,2,2,8,256]{4,3,2,1,0:T(8,128)S(1)} async-done(((f32[8,2,2,8,256]{4,3,2,1,0:T(8,128)}), f32[8,2,2,8,256]{4,3,2,1,0:T(8,128)S(1)}, u32[]{:S(2)}, u32[]{:S(2)}) %all-to-all-start) | async-done | bytes 262176 | tf_op jit(solution)/shard_map/all_to_all | solution.py:165
  27.9 0.0 copy-start
  27.9 12.4 %all_to_all.10.forces_ref = f32[8,3,2,8,256]{4,3,2,1,0:T(8,128)} all-to-all(f32[8,3,2,8,256]{4,3,2,1,0:T(8,128)} %spread_patches.1), channel_id=1, replica_groups=mesh['sec'=8,'tile'=4] {'sec'}, dimensions={0} | all-to-all | bytes 786432 | tf_op jit(solution)/shard_map/all_to_all | solution.py:156
  40.3 0.0 copy-done
  40.3 2.6 %cross_steps.1 = f32[2,16,8,256]{3,2,1,0:T(8,128)} custom-call(f32[8,2,2,8,256]{4,3,2,1,0:T(8,128)} %copy-done, f32[8,3,2,8,256]{4,3,2,1,0:T(8,128)} %all_to_all.10.forces_ref, f32[16,8,256]{2,1,0:T(8,128)} %stiff_ref.3), custom_call_target="tpu_custom_call" | custom-call | flops 10000000 | bytes 800000 | tf_op jit(solution)/shard_map/cross_steps/pallas_call | solution.py:166
  (2 shorter events, 0.0 us)
Async XLA Ops:
  1.5 6.7 %collective-permute-start = (f32[3,2,8,256]{3,2,1,0:T(8,128)S(1)}, f32[3,2,8,256]{3,2,1,0:T(8,128)S(1)}, u32[]{:S(2)}, u32[]{:S(2)}) collective-permute-start(f32[3,2,8,256]{3,2,1,0:T(8,128)S(1)} %pad_maximum_fusion), channel_id=1, source_target_pairs={{0,1},{1,2},{2,3},{4,5},{5,6},{6,7},{8,9},{9,10},{10,11},{12,13},{... | collective-permute-start | bytes 147464 | tf_op jit(solution)/shard_map/ppermute | solution.py:141
  6.5 6.0 %collective-permute-start.1 = (f32[3,2,8,256]{3,2,1,0:T(8,128)S(1)}, f32[3,2,8,256]{3,2,1,0:T(8,128)S(1)}, u32[]{:S(2)}, u32[]{:S(2)}) collective-permute-start(f32[3,2,8,256]{3,2,1,0:T(8,128)S(1)} %pad_maximum_fusion.1), channel_id=1, source_target_pairs={{1,0},{2,1},{3,2},{5,4},{6,5},{7,6},{9,8},{10,9},{11,10},{13,12},{... | collective-permute-start | bytes 147464 | tf_op jit(solution)/shard_map/ppermute | solution.py:142
  8.2 4.3 %copy-start.1 = (f32[3,2,8,256]{3,2,1,0:T(8,128)}, f32[3,2,8,256]{3,2,1,0:T(8,128)S(1)}, u32[]{:S(2)}) copy-start(f32[3,2,8,256]{3,2,1,0:T(8,128)S(1)} %collective-permute-done.before_ref) | copy-start | bytes 147460
  12.5 0.6 %copy-start.2 = (f32[3,2,8,256]{3,2,1,0:T(8,128)}, f32[3,2,8,256]{3,2,1,0:T(8,128)S(1)}, u32[]{:S(2)}) copy-start(f32[3,2,8,256]{3,2,1,0:T(8,128)S(1)} %collective-permute-done.1.after_ref) | copy-start | bytes 147460
  17.2 10.7 %all-to-all-start = ((f32[8,2,2,8,256]{4,3,2,1,0:T(8,128)}), f32[8,2,2,8,256]{4,3,2,1,0:T(8,128)S(1)}, u32[]{:S(2)}, u32[]{:S(2)}) async-start(f32[8,2,2,8,256]{4,3,2,1,0:T(8,128)} %plane_steps.1), calls=%async_computation | async-start | bytes 524288 | tf_op jit(solution)/shard_map/all_to_all | solution.py:165
  27.9 12.4 %copy-start = (f32[8,2,2,8,256]{4,3,2,1,0:T(8,128)}, f32[8,2,2,8,256]{4,3,2,1,0:T(8,128)S(1)}, u32[]{:S(2)}) copy-start(f32[8,2,2,8,256]{4,3,2,1,0:T(8,128)S(1)} %all-to-all-done.moved_ref) | copy-start | bytes 786436

commit v3 on v1

--- a/solution.py
+++ b/solution.py
@@ -17,6 +17,8 @@
 HALO = -(-(ISTEPS - 1) // 8) * 8
 
 VMEM = pl.BlockSpec(memory_space=pltpu.VMEM)
+HBM = pl.BlockSpec(memory_space=pltpu.HBM)
+ANY = pl.BlockSpec(memory_space=pl.ANY)
 
 
 def spread_kernel(layers, inner_rows, blocks, dest_ref, pos_ref, flow_ref, conf_ref, out_ref):
@@ -58,58 +60,117 @@
     return left, right
 
 
-def plane_kernel(force_ref, stiff_ref, before_ref, after_ref, forces_ref, out_ref):
+def start_all(copies):
+    for copy in copies:
+        copy.start()
+    return copies
+
+
+def wait_all(copies):
+    for copy in copies:
+        copy.wait()
+
+
+def edge_kernel(force_ref, stiff_ref, first_ref, last_ref, sems):
+    rows = stiff_ref.shape[1]
+    copies = []
+    for start, out_ref in ((0, first_ref), (rows - HALO, last_ref)):
+        span = pl.ds(start, HALO)
+        copies.append(pltpu.make_async_copy(force_ref.at[:, :, span], out_ref.at[pl.ds(0, 2)], sems.at[len(copies)]))
+        copies.append(pltpu.make_async_copy(stiff_ref.at[:, span], out_ref.at[2], sems.at[len(copies)]))
+    wait_all(start_all(copies))
+
+
+def plane_kernel(force_ref, stiff_ref, before_ref, after_ref, order_ref, out_ref, held, done, sems):
     _, layers, rows, columns = force_ref.shape
-    out_ref[:, 2:] = forces_ref[...]
     groups = out_ref.shape[0]
     inner_rows = rows // groups
-    width = 128
+    width = held.shape[-1]
     total = rows + 2 * HALO
-    lane = lax.broadcasted_iota(jnp.int32, (total, width), 1)
-    spans = [slice(i * width, (i + 1) * width) for i in range(columns // width)]
+    stride = total // 8
+    blocks = columns // width
+    copies = []
+    for b in range(blocks):
+        span = pl.ds(b * width, width)
+        for source, start, length in (
+            (before_ref.at[:, :, :, span], 0, HALO),
+            (after_ref.at[:, :, :, span], HALO + rows, HALO),
+        ):
+            target = held.at[:, :, b, pl.ds(start, length)]
+            copies.append(pltpu.make_async_copy(source, target, sems.at[len(copies)]))
+        own = pl.ds(HALO, rows)
+        copies.append(
+            pltpu.make_async_copy(force_ref.at[:, :, :, span], held.at[pl.ds(0, 2), :, b, own], sems.at[len(copies)])
+        )
+        copies.append(pltpu.make_async_copy(stiff_ref.at[:, :, span], held.at[2, :, b, own], sems.at[len(copies)]))
+    wait_all(start_all(copies))
+    lane = lax.broadcasted_iota(jnp.int32, (8, width), 1)
+
+    def rows_of(c, l):
+        return [
+            [STEP_PLANE * held[c, l, b, pl.ds(j, 8, stride=stride), :] for b in range(blocks)] for j in range(stride)
+        ]
+
     for l in range(layers):
-        spring, keep = [], []
-        for span in spans:
-            k = STEP_PLANE * jnp.concatenate(
-                [before_ref[2, l, :, span], stiff_ref[l, :, span], after_ref[2, l, :, span]], axis=0
-            )
-            spring.append(k)
-            keep.append(1.0 - 4.0 * k)
+        spring = rows_of(2, l)
+        keep = [[1.0 - 4.0 * k for k in row] for row in spring]
         for c in range(2):
-            push = [
-                STEP_PLANE
-                * jnp.concatenate(
-                    [before_ref[c, l, :, span], force_ref[c, l, :, span], after_ref[c, l, :, span]], axis=0
-                )
-                for span in spans
-            ]
+            push = rows_of(c, l)
             field = push
             for step in range(1, ISTEPS):
-                left, right = shifted(field, lane, width)
-                field = [
-                    k * (pltpu.roll(x, 1, 0) + pltpu.roll(x, total - 1, 0) + a + b) + (g * x + f)
-                    for x, a, b, k, g, f in zip(field, left, right, spring, keep, push)
-                ]
-            for span, x in zip(spans, field):
+                above = [[pltpu.roll(x, 1, 0) for x in field[-1]]] + field[:-1]
+                below = field[1:] + [[pltpu.roll(x, 7, 0) for x in field[0]]]
+                moved = []
+                for j in range(stride):
+                    left, right = shifted(field[j], lane, width)
+                    moved.append(
+                        [
+                            k * ((u + d) + (a + b)) + (g * x + f)
+                            for x, u, d, a, b, k, g, f in zip(
+                                field[j], above[j], below[j], left, right, spring[j], keep[j], push[j]
+                            )
+                        ]
+                    )
+                field = moved
+            for j in range(stride):
+                for b in range(blocks):
+                    done[c, l, b, pl.ds(j, 8, stride=stride), :] = field[j][b]
+            for b in range(blocks):
                 for o in range(groups):
-                    start = HALO + o * inner_rows
-                    out_ref[o, c, l, :, span] = x[start : start + inner_rows]
-
-
-def cross_kernel(moved_ref, stiff_ref, out_ref):
+                    out_ref[o, c, l, :, b * width : (b + 1) * width] = done[
+                        c, l, b, HALO + o * inner_rows : HALO + (o + 1) * inner_rows, :
+                    ]
+
+
+def cross_kernel(moved_ref, forces_ref, stiff_ref, out_ref, held, spring_held, result, sems, out_sems):
     groups, _, layers, inner_rows, columns = moved_ref.shape
     sections = groups * layers
-    width = 128
+    width = held.shape[-1]
+    blocks = columns // width
     zero = jnp.zeros((1, inner_rows, width), jnp.float32)
-    for i in range(columns // width):
-        span = slice(i * width, (i + 1) * width)
+    copies = []
+    for b in range(blocks):
+        span = pl.ds(b * width, width)
+        pieces = [(stiff_ref.at[:, :, span], spring_held.at[b])]
+        pieces += [(forces_ref.at[:, c, :, :, span], held.at[b, 2 + c]) for c in (2, 0)]
+        pieces += [(moved_ref.at[:, 0, :, :, span], held.at[b, 0])]
+        pieces += [(forces_ref.at[:, 1, :, :, span], held.at[b, 3]), (moved_ref.at[:, 1, :, :, span], held.at[b, 1])]
+        copies.append(
+            start_all([pltpu.make_async_copy(source, target, sems.at[b, i]) for i, (source, target) in enumerate(pieces)])
+        )
+    outgoing = []
+    for b in range(blocks):
+        span = pl.ds(b * width, width)
 
         def channel(c):
-            return moved_ref[:, c, :, :, span].reshape(sections, inner_rows, width)
-
-        spring = STEP_CROSS * stiff_ref[:, :, span]
+            return held[b, c].reshape(sections, inner_rows, width)
+
+        wait_all(copies[b][:4])
+        spring = STEP_CROSS * spring_held[b]
         weight = STEP_CROSS * channel(4)
         for c in range(2):
+            if c:
+                wait_all(copies[b][4:])
             pull = STEP_CROSS * channel(2 + c)
             field = channel(c)
             for step in range(ZSTEPS):
@@ -118,7 +179,11 @@
                 stretch = pull - weight * rise
                 stretch_above = jnp.concatenate([stretch[1:], zero], axis=0)
                 field = field + (spring * (rise_above - rise) + (stretch - stretch_above))
-            out_ref[c, :, :, span] = field
+            result[b, c] = field
+            outgoing += start_all(
+                [pltpu.make_async_copy(result.at[b, c], out_ref.at[c, :, :, span], out_sems.at[b, c])]
+            )
+    wait_all(outgoing)
 
 
 def per_device(
@@ -134,13 +199,18 @@
     up = [(i, i + 1) for i in range(tiles - 1)]
     down = [(j, i) for i, j in up]
 
-    def edge(start):
-        return jnp.concatenate(
-            [in_plane_force[:, :, start : start + HALO], stiffness[None, :, start : start + HALO]], axis=0
-        )
-
-    before = lax.ppermute(edge(rows - HALO), "tile", up)
-    after = lax.ppermute(edge(0), "tile", down)
+    edge_shape = jax.ShapeDtypeStruct((3, layers, HALO, columns), jnp.float32)
+    first, last = pl.pallas_call(
+        edge_kernel,
+        out_shape=[edge_shape] * 2,
+        in_specs=[HBM] * 2,
+        out_specs=[ANY] * 2,
+        scratch_shapes=[pltpu.SemaphoreType.DMA((4,))],
+        cost_estimate=pl.CostEstimate(flops=0, bytes_accessed=200000, transcendentals=0),
+        name="pack_edges",
+    )(in_plane_force, stiffness)
+    before = lax.ppermute(last, "tile", up)
+    after = lax.ppermute(first, "tile", down)
     forces = pl.pallas_call(
         functools.partial(spread_kernel, layers, inner_rows, blocks),
         out_shape=jax.ShapeDtypeStruct((groups, 3, layers, inner_rows, columns), jnp.float32),
@@ -154,23 +224,36 @@
         patch_flow.reshape(count * 2, width),
         patch_conf.reshape(count, width),
     )
-    mixed = pl.pallas_call(
+    moved_forces = lax.all_to_all(forces, "sec", split_axis=0, concat_axis=0, tiled=True)
+    planar = pl.pallas_call(
         plane_kernel,
-        out_shape=jax.ShapeDtypeStruct((groups, 5, layers, inner_rows, columns), jnp.float32),
-        in_specs=[VMEM] * 5,
+        out_shape=jax.ShapeDtypeStruct((groups, 2, layers, inner_rows, columns), jnp.float32),
+        in_specs=[HBM] * 2 + [ANY] * 3,
         out_specs=VMEM,
-        cost_estimate=pl.CostEstimate(flops=10000000, bytes_accessed=800000, transcendentals=0),
+        scratch_shapes=[
+            pltpu.VMEM((3, layers, blocks, rows + 2 * HALO, width), jnp.float32),
+            pltpu.VMEM((2, layers, blocks, rows + 2 * HALO, width), jnp.float32),
+            pltpu.SemaphoreType.DMA((4 * blocks,)),
+        ],
+        cost_estimate=pl.CostEstimate(flops=10000000, bytes_accessed=10000000, transcendentals=0),
         name="plane_steps",
     )(in_plane_force, stiffness, before, after, forces)
-    moved = lax.all_to_all(mixed, "sec", split_axis=0, concat_axis=0, tiled=True)
+    moved = lax.all_to_all(planar, "sec", split_axis=0, concat_axis=0, tiled=True)
     return pl.pallas_call(
         cross_kernel,
         out_shape=jax.ShapeDtypeStruct((2, groups * layers, inner_rows, columns), jnp.float32),
-        in_specs=[VMEM] * 2,
-        out_specs=VMEM,
+        in_specs=[ANY] * 2 + [HBM],
+        out_specs=HBM,
+        scratch_shapes=[
+            pltpu.VMEM((blocks, 5, groups, layers, inner_rows, width), jnp.float32),
+            pltpu.VMEM((blocks, groups * layers, inner_rows, width), jnp.float32),
+            pltpu.VMEM((blocks, 2, groups * layers, inner_rows, width), jnp.float32),
+            pltpu.SemaphoreType.DMA((blocks, 6)),
+            pltpu.SemaphoreType.DMA((blocks, 2)),
+        ],
         cost_estimate=pl.CostEstimate(flops=10000000, bytes_accessed=800000, transcendentals=0),
         name="cross_steps",
-    )(moved, stiffness_z)
+    )(moved, moved_forces, stiffness_z)
 
 
 def solution(mesh):

time: 35.9 us -> 44.8 us (1.25)
  blocking collectives: 15.3 us -> 22.5 us
  Pallas kernels: 9.19 us -> 12.2 us
  local copies, waits for them, and re-layouts: 2.14 us -> 0.63 us
    all_to_all x1 -> x2, blocking collectives: 15.3 us -> 22.5 us  [the longest x1 11.4 us: per_device(): lax.all_to_all(forces, 'sec', split_axis=0, concat_axis=0, tiled=True)]
    pallas_call x1 -> x2, Pallas kernels: 4.47 us -> 7.76 us  [the longest x1 4.11 us: per_device(): pl.pallas_call(edge_kernel, out_shape=[edge_shape] * 2, in_specs=[HBM] *...]
    slice x1 -> x0, local copies, waits for them, and re-layouts: 0.78 us -> none  [edge(): in_plane_force[:, :, start:start + HALO]]
    broadcast_in_dim x1 -> x0, local copies, waits for them, and re-layouts: 0.74 us -> none  [edge(): stiffness[None, :, start:start + HALO]]
  transfers between devices with their start and end apart: 2 -> 2, of which waited for: 1 -> 1; matrix products, arithmetic and copies ran while one was open for 0% -> 0% of each run, Pallas kernels for 6% -> 5%
where the time goes in v3:
time: 44.8 us; the launch traced here: 44.4 us
  blocking collectives  22.5 us (50%)
  Pallas kernels  12.2 us (27%)
  starting transfers between devices  6.22 us (14%)
  waiting for transfers between devices  2.74 us (6%)
  local copies, waits for them, and re-layouts  0.63 us (1%)
    all_to_all x1, blocking collectives, per_device(): lax.all_to_all(forces, 'sec', split_axis=0, concat_axis=0, tiled=True)  11.4 us
    all_to_all x1, blocking collectives, per_device(): lax.all_to_all(planar, 'sec', split_axis=0, concat_axis=0, tiled=True)  11.1 us
    ppermute x1, starting transfers between devices, per_device(): before = lax.ppermute(last, 'tile', up)  4.93 us
    pallas_call x1, Pallas kernels, per_device(): pl.pallas_call(edge_kernel, out_shape=[edge_shape] * 2, in_specs=[HBM] *...  4.11 us
    pallas_call x1, Pallas kernels, per_device(): pl.pallas_call(plane_kernel, out_shape=jax.ShapeDtypeStruct((groups, 2, l...  3.65 us
    ppermute x1, waiting for transfers between devices, per_device(): after = lax.ppermute(first, 'tile', down)  2.74 us
    pallas_call x1, Pallas kernels, per_device(): pl.pallas_call(cross_kernel, out_shape=jax.ShapeDtypeStruct((2, groups *...  2.34 us
    pallas_call x1, Pallas kernels, per_device(): pl.pallas_call(functools.partial(spread_kernel, layers, inner_rows, block...  2.15 us
  transfers between devices with their start and end apart: 2, of which 1 were waited for; matrix products, arithmetic and copies ran while one was open for 0% of the time, Pallas kernels for 5%

profile of v3, /device:TPU:0, one launch (start us, length us, event | category | flops | bytes accessed | tf_op | source)
XLA Modules:
  0.0 44.4 jit_solution(9672584156073345596)
XLA Ops:
  0.0 4.1 %pack_edges.1 = (f32[3,2,8,256]{3,2,1,0:T(8,128)}, f32[3,2,8,256]{3,2,1,0:T(8,128)}) custom-call(f32[2,2,64,256]{3,2,1,0:T(8,128)} %force_ref.3, f32[2,64,256]{2,1,0:T(8,128)} %stiff_ref.4), custom_call_target="tpu_custom_call" | custom-call | bytes 200000 | tf_op jit(solution)/shard_map/pack_edges/pallas_call | solution.py:203
  4.1 4.9 %collective-permute-start = (f32[3,2,8,256]{3,2,1,0:T(8,128)}, f32[3,2,8,256]{3,2,1,0:T(8,128)S(1)}, u32[]{:S(2)}, u32[]{:S(2)}) collective-permute-start(f32[3,2,8,256]{3,2,1,0:T(8,128)} %get-tuple-element.7), channel_id=1, source_target_pairs={{0,1},{1,2},{2,3},{4,5},{5,6},{6,7},{8,9},{9,10},{10,11},{12,13},{... | collective-permute-start | bytes 147464 | tf_op jit(solution)/shard_map/ppermute | solution.py:212
  9.1 1.3 %collective-permute-start.1 = (f32[3,2,8,256]{3,2,1,0:T(8,128)}, f32[3,2,8,256]{3,2,1,0:T(8,128)S(1)}, u32[]{:S(2)}, u32[]{:S(2)}) collective-permute-start(f32[3,2,8,256]{3,2,1,0:T(8,128)} %get-tuple-element.8), channel_id=1, source_target_pairs={{1,0},{2,1},{3,2},{5,4},{6,5},{7,6},{9,8},{10,9},{11,10},{13,12},{... | collective-permute-start | bytes 147464 | tf_op jit(solution)/shard_map/ppermute | solution.py:213
  10.4 2.1 %spread_patches.1.order_ref = f32[8,3,2,8,256]{4,3,2,1,0:T(8,128)} custom-call(s32[1,256]{1,0:T(1,128)} %bitcast.6, s32[1,256]{1,0:T(1,128)} %bitcast.7, f32[512,128]{1,0:T(8,128)} %bitcast.4, f32[256,128]{1,0:T(8,128)} %bitcast.5), custom_call_target="tpu_custom_call" | custom-call | flops 150994944 | bytes 800000 | tf_op jit(solution)/shard_map/spread_patches/pallas_call | solution.py:214
  12.5 0.0 collective-permute-done.before_ref
  12.5 0.0 copy-start.1
  12.5 2.7 %collective-permute-done.1.after_ref = f32[3,2,8,256]{3,2,1,0:T(8,128)S(1)} collective-permute-done((f32[3,2,8,256]{3,2,1,0:T(8,128)}, f32[3,2,8,256]{3,2,1,0:T(8,128)S(1)}, u32[]{:S(2)}, u32[]{:S(2)}) %collective-permute-start.1) | collective-permute-done | bytes 49184 | tf_op jit(solution)/shard_map/ppermute | solution.py:213
  15.3 0.0 copy-done.1
  15.3 0.0 copy-start.2
  15.3 0.6 %copy-done.2 = f32[3,2,8,256]{3,2,1,0:T(8,128)} copy-done((f32[3,2,8,256]{3,2,1,0:T(8,128)}, f32[3,2,8,256]{3,2,1,0:T(8,128)S(1)}, u32[]{:S(2)}) %copy-start.2) | copy-done | bytes 49176
  15.9 3.6 %plane_steps.1 = f32[8,2,2,8,256]{4,3,2,1,0:T(8,128)} custom-call(f32[2,2,64,256]{3,2,1,0:T(8,128)} %force_ref.3, f32[2,64,256]{2,1,0:T(8,128)} %stiff_ref.4, f32[3,2,8,256]{3,2,1,0:T(8,128)} %copy-done.1, f32[3,2,8,256]{3,2,1,0:T(8,128)} %copy-done.2, f32[8,3,2,8,256]{4,3,2,1,0:T(8,128)} %spread_patches.1.order_ref), custom_call_target="tpu_custom_call" | custom-call | flops 10000000 | bytes 10000000 | tf_op jit(solution)/shard_map/plane_steps/pallas_call | solution.py:228
  19.5 0.0 copy-start
  19.5 11.1 %all_to_all.10.moved_ref = f32[8,2,2,8,256]{4,3,2,1,0:T(8,128)} all-to-all(f32[8,2,2,8,256]{4,3,2,1,0:T(8,128)} %plane_steps.1), channel_id=1, replica_groups=mesh['sec'=8,'tile'=4] {'sec'}, dimensions={0} | all-to-all | bytes 524288 | tf_op jit(solution)/shard_map/all_to_all | solution.py:241
  30.6 0.0 copy-done
  30.6 11.4 %all_to_all.11.forces_ref = f32[8,3,2,8,256]{4,3,2,1,0:T(8,128)} all-to-all(f32[8,3,2,8,256]{4,3,2,1,0:T(8,128)S(1)} %copy-done), channel_id=1, replica_groups=mesh['sec'=8,'tile'=4] {'sec'}, dimensions={0} | all-to-all | bytes 786432 | tf_op jit(solution)/shard_map/all_to_all | solution.py:227
  42.1 2.3 %cross_steps.1 = f32[2,16,8,256]{3,2,1,0:T(8,128)} custom-call(f32[8,2,2,8,256]{4,3,2,1,0:T(8,128)} %all_to_all.10.moved_ref, f32[8,3,2,8,256]{4,3,2,1,0:T(8,128)} %all_to_all.11.forces_ref, f32[16,8,256]{2,1,0:T(8,128)} %stiff_ref.5), custom_call_target="tpu_custom_call" | custom-call | flops 10000000 | bytes 800000 | tf_op jit(solution)/shard_map/cross_steps/pallas_call | solution.py:242
Async XLA Ops:
  4.1 8.4 %collective-permute-start = (f32[3,2,8,256]{3,2,1,0:T(8,128)}, f32[3,2,8,256]{3,2,1,0:T(8,128)S(1)}, u32[]{:S(2)}, u32[]{:S(2)}) collective-permute-start(f32[3,2,8,256]{3,2,1,0:T(8,128)} %get-tuple-element.7), channel_id=1, source_target_pairs={{0,1},{1,2},{2,3},{4,5},{5,6},{6,7},{8,9},{9,10},{10,11},{12,13},{... | collective-permute-start | bytes 147464 | tf_op jit(solution)/shard_map/ppermute | solution.py:212
  9.1 6.2 %collective-permute-start.1 = (f32[3,2,8,256]{3,2,1,0:T(8,128)}, f32[3,2,8,256]{3,2,1,0:T(8,128)S(1)}, u32[]{:S(2)}, u32[]{:S(2)}) collective-permute-start(f32[3,2,8,256]{3,2,1,0:T(8,128)} %get-tuple-element.8), channel_id=1, source_target_pairs={{1,0},{2,1},{3,2},{5,4},{6,5},{7,6},{9,8},{10,9},{11,10},{13,12},{... | collective-permute-start | bytes 147464 | tf_op jit(solution)/shard_map/ppermute | solution.py:213
  12.5 2.7 %copy-start.1 = (f32[3,2,8,256]{3,2,1,0:T(8,128)}, f32[3,2,8,256]{3,2,1,0:T(8,128)S(1)}, u32[]{:S(2)}) copy-start(f32[3,2,8,256]{3,2,1,0:T(8,128)S(1)} %collective-permute-done.before_ref) | copy-start | bytes 147460
  15.3 0.6 %copy-start.2 = (f32[3,2,8,256]{3,2,1,0:T(8,128)}, f32[3,2,8,256]{3,2,1,0:T(8,128)S(1)}, u32[]{:S(2)}) copy-start(f32[3,2,8,256]{3,2,1,0:T(8,128)S(1)} %collective-permute-done.1.after_ref) | copy-start | bytes 147460
  19.5 11.1 %copy-start = (f32[8,3,2,8,256]{4,3,2,1,0:T(8,128)S(1)}, f32[8,3,2,8,256]{4,3,2,1,0:T(8,128)}, u32[]{:S(2)}) copy-start(f32[8,3,2,8,256]{4,3,2,1,0:T(8,128)} %spread_patches.1.order_ref) | copy-start | bytes 1179652

commit v4 on v3

v4 whole, which is shorter than its diff:
```python
import functools

import jax
import jax.numpy as jnp
from jax import lax
from jax.experimental import pallas as pl
from jax.experimental.pallas import tpu as pltpu
from jax.sharding import PartitionSpec as P

ISTEPS = 8
ZSTEPS = 8


STEP_PLANE = 0.12
STEP_CROSS = 0.15

HALO = -(-(ISTEPS - 1) // 8) * 8

VMEM = pl.BlockSpec(memory_space=pltpu.VMEM)
LIMIT = pltpu.CompilerParams(vmem_limit_bytes=8 * 1024 * 1024)
ANY = pl.BlockSpec(memory_space=pl.ANY)


def spread_kernel(layers, inner_rows, blocks, dest_ref, pos_ref, flow_ref, conf_ref, out_ref):
    groups = out_ref.shape[0]
    count, width = conf_ref.shape
    place = pos_ref[...]
    layer = place // (inner_rows * blocks)
    inner_row = place // blocks % inner_rows
    column_block = place % blocks
    slot = (dest_ref[...] * layers + layer) * inner_rows + inner_row
    slots = groups * layers * inner_rows
    conf = conf_ref[...]
    terms = [flow_ref[pl.ds(c, count, stride=2), :] * conf for c in range(2)] + [conf]
    rest = jnp.concatenate(terms, axis=1)
    parts = []
    for _ in range(3):
        parts.append(rest.astype(jnp.bfloat16))
        rest = rest - parts[-1].astype(jnp.float32)
    numbers = lax.broadcasted_iota(jnp.int32, (slots, count), 0)
    for b in range(blocks):
        key = jnp.where(column_block == b, slot, -1)
        hit = jnp.where(numbers == key, 1.0, 0.0).astype(jnp.bfloat16)
        total = sum(jnp.dot(hit, part, preferred_element_type=jnp.float32) for part in reversed(parts))
        for o in range(groups):
            for l in range(layers):
                start = (o * layers + l) * inner_rows
                for c in range(3):
                    out_ref[o, c, l, :, b * width : (b + 1) * width] = total[
                        start : start + inner_rows, c * width : (c + 1) * width
                    ]


def shifted(blocks, lane, width):
    ahead = [pltpu.roll(x, width - 1, 1) for x in blocks]
    behind = [pltpu.roll(x, 1, 1) for x in blocks]
    zero = jnp.zeros_like(blocks[0])
    right = [jnp.where(lane == width - 1, after, own) for own, after in zip(ahead, ahead[1:] + [zero])]
    left = [jnp.where(lane == 0, before, own) for own, before in zip(behind, [zero] + behind[:-1])]
    return left, right


def start_all(copies):
    for copy in copies:
        copy.start()
    return copies


def wait_all(copies):
    for copy in copies:
        copy.wait()


def edge_kernel(force_ref, stiff_ref, first_ref, last_ref, sems):
    rows = stiff_ref.shape[1]
    copies = []
    for start, out_ref in ((0, first_ref), (rows - HALO, last_ref)):
        span = pl.ds(start, HALO)
        copies.append(pltpu.make_async_copy(force_ref.at[:, :, span], out_ref.at[pl.ds(0, 2)], sems.at[len(copies)]))
        copies.append(pltpu.make_async_copy(stiff_ref.at[:, span], out_ref.at[2], sems.at[len(copies)]))
    wait_all(start_all(copies))


def plane_kernel(force_ref, stiff_ref, before_ref, after_ref, forces_ref, out_ref, held, coefs, done, sems):
    _, layers, rows, columns = force_ref.shape
    groups = out_ref.shape[0]
    inner_rows = rows // groups
    width = held.shape[-1]
    total = rows + 2 * HALO
    stride = total // 8
    blocks = columns // width
    copies = []
    for b in range(blocks):
        span = pl.ds(b * width, width)
        for source, start, length in (
            (before_ref.at[:, :, :, span], 0, HALO),
            (after_ref.at[:, :, :, span], HALO + rows, HALO),
        ):
            target = held.at[:, :, b, pl.ds(start, length)]
            copies.append(pltpu.make_async_copy(source, target, sems.at[len(copies)]))
        own = pl.ds(HALO, rows)
        copies.append(
            pltpu.make_async_copy(force_ref.at[:, :, :, span], held.at[pl.ds(0, 2), :, b, own], sems.at[len(copies)])
        )
        copies.append(pltpu.make_async_copy(stiff_ref.at[:, :, span], held.at[2, :, b, own], sems.at[len(copies)]))
    start_all(copies)
    passed = start_all([pltpu.make_async_copy(forces_ref, out_ref.at[:, pl.ds(2, 3)], sems.at[len(copies)])])
    wait_all(copies)
    lane = lax.broadcasted_iota(jnp.int32, (8, width), 1)
    places = [(j, b) for j in range(stride) for b in range(blocks)]

    def one(index, carry):
        l, c = index // 2, index % 2
        field = []
        for n, (j, b) in enumerate(places):
            k = STEP_PLANE * held[2, l, b, pl.ds(j, 8, stride=stride), :]
            f = STEP_PLANE * held[c, l, b, pl.ds(j, 8, stride=stride), :]
            coefs[0, n] = k
            coefs[1, n] = 1.0 - 4.0 * k
            coefs[2, n] = f
            field.append(f)

        def step(_, flat):
            field = [flat[j * blocks : (j + 1) * blocks] for j in range(stride)]
            above = [[pltpu.roll(x, 1, 0) for x in field[-1]]] + field[:-1]
            below = field[1:] + [[pltpu.roll(x, 7, 0) for x in field[0]]]
            moved = []
            for j in range(stride):
                left, right = shifted(field[j], lane, width)
                for b in range(blocks):
                    n = len(moved)
                    near = (above[j][b] + below[j][b]) + (left[b] + right[b])
                    moved.append(coefs[0, n] * near + (coefs[1, n] * field[j][b] + coefs[2, n]))
            return moved

        field = lax.fori_loop(1, ISTEPS, step, field)
        for x, (j, b) in zip(field, places):
            done[b, pl.ds(j, 8, stride=stride), :] = x
        for b in range(blocks):
            for o in range(groups):
                out_ref[o, c, l, :, b * width : (b + 1) * width] = done[
                    b, HALO + o * inner_rows : HALO + (o + 1) * inner_rows, :
                ]
        return carry

    lax.fori_loop(0, 2 * layers, one, 0)
    wait_all(passed)


def cross_kernel(moved_ref, stiff_ref, out_ref, result, sems):
    groups, _, layers, inner_rows, columns = moved_ref.shape
    sections = groups * layers
    width = result.shape[-1]
    blocks = columns // width
    zero = jnp.zeros((1, inner_rows, width), jnp.float32)

    def outgoing(index):
        b, c = index // 2, index % 2
        span = pl.ds(pl.multiple_of(b * width, width), width)
        return pltpu.make_async_copy(result.at[index], out_ref.at[c, :, :, span], sems.at[index])

    def one(index, carry):
        b, c = index // 2, index % 2
        span = pl.ds(pl.multiple_of(b * width, width), width)

        def channel(c):
            return moved_ref[:, c, :, :, span].reshape(sections, inner_rows, width)

        spring = STEP_CROSS * stiff_ref[:, :, span]
        weight = STEP_CROSS * channel(4)
        pull = STEP_CROSS * channel(2 + c)

        def step(_, field):
            rise = field - jnp.concatenate([zero, field[:-1]], axis=0)
            rise_above = jnp.concatenate([rise[1:], -field[-1:]], axis=0)
            stretch = pull - weight * rise
            stretch_above = jnp.concatenate([stretch[1:], zero], axis=0)
            return field + (spring * (rise_above - rise) + (stretch - stretch_above))

        result[index] = lax.fori_loop(0, ZSTEPS, step, channel(c))
        outgoing(index).start()
        return carry

    lax.fori_loop(0, 2 * blocks, one, 0)
    for index in range(2 * blocks):
        outgoing(index).wait()


def per_device(
    in_plane_force, stiffness, stiffness_z, patch_dest, patch_pos, patch_flow, patch_conf
):
    groups = lax.axis_size("sec")
    tiles = lax.axis_size("tile")
    layers, rows, columns = stiffness.shape
    inner_rows = rows // groups
    width = patch_flow.shape[-1]
    blocks = columns // width
    count = patch_pos.shape[2]
    up = [(i, i + 1) for i in range(tiles - 1)]
    down = [(j, i) for i, j in up]

    edge_shape = jax.ShapeDtypeStruct((3, layers, HALO, columns), jnp.float32)
    first, last = pl.pallas_call(
        edge_kernel,
        out_shape=[edge_shape] * 2,
        in_specs=[ANY] * 2,
        out_specs=[ANY] * 2,
        scratch_shapes=[pltpu.SemaphoreType.DMA((4,))],
        compiler_params=LIMIT,
        cost_estimate=pl.CostEstimate(flops=0, bytes_accessed=200000, transcendentals=0),
        name="pack_edges",
    )(in_plane_force, stiffness)
    before = lax.ppermute(last, "tile", up)
    after = lax.ppermute(first, "tile", down)
    forces = pl.pallas_call(
        functools.partial(spread_kernel, layers, inner_rows, blocks),
        out_shape=jax.ShapeDtypeStruct((groups, 3, layers, inner_rows, columns), jnp.float32),
        in_specs=[VMEM] * 4,
        out_specs=VMEM,
        compiler_params=LIMIT,
        cost_estimate=pl.CostEstimate(flops=6 * 256 * 256 * 384, bytes_accessed=800000, transcendentals=0),
        name="spread_patches",
    )(
        patch_dest.reshape(1, count),
        patch_pos.reshape(1, count),
        patch_flow.reshape(count * 2, width),
        patch_conf.reshape(count, width),
    )
    mixed = pl.pallas_call(
        plane_kernel,
        out_shape=jax.ShapeDtypeStruct((groups, 5, layers, inner_rows, columns), jnp.float32),
        in_specs=[ANY] * 5,
        out_specs=VMEM,
        scratch_shapes=[
            pltpu.VMEM((3, layers, blocks, rows + 2 * HALO, width), jnp.float32),
            pltpu.VMEM((3, (rows + 2 * HALO) // 8 * blocks, 8, width), jnp.float32),
            pltpu.VMEM((blocks, rows + 2 * HALO, width), jnp.float32),
            pltpu.SemaphoreType.DMA((4 * blocks + 1,)),
        ],
        compiler_params=LIMIT,
        cost_estimate=pl.CostEstimate(flops=10000000, bytes_accessed=10000000, transcendentals=0),
        name="plane_steps",
    )(in_plane_force, stiffness, before, after, forces)
    moved = lax.all_to_all(mixed, "sec", split_axis=0, concat_axis=0, tiled=True)
    return pl.pallas_call(
        cross_kernel,
        out_shape=jax.ShapeDtypeStruct((2, groups * layers, inner_rows, columns), jnp.float32),
        in_specs=[VMEM] * 2,
        out_specs=ANY,
        scratch_shapes=[
            pltpu.VMEM((2 * blocks, groups * layers, inner_rows, width), jnp.float32),
            pltpu.SemaphoreType.DMA((2 * blocks,)),
        ],
        compiler_params=LIMIT,
        cost_estimate=pl.CostEstimate(flops=10000000, bytes_accessed=800000, transcendentals=0),
        name="cross_steps",
    )(moved, stiffness_z)


def solution(mesh):
    placed = (
        P(None, "sec", "tile", None),
        P("sec", "tile", None),
        P(None, ("tile", "sec"), None),
        P("sec", "tile", None, None),
        P("sec", "tile", None),
        P("sec", "tile", None, None, None),
        P("sec", "tile", None, None),
    )
    return jax.shard_map(
        per_device,
        mesh=mesh,
        in_specs=placed,
        out_specs=P(None, None, ("tile", "sec"), None),
        check_vma=False,
    )
```

time: 44.8 us -> 33.3 us (0.74)
  blocking collectives: 22.5 us -> 14.8 us
  Pallas kernels: 12.2 us -> 5.64 us
  local copies, waits for them, and re-layouts: 0.63 us -> 2.54 us
  waiting for transfers between devices: 2.74 us -> 3.57 us
    all_to_all x2 -> x1, blocking collectives: 22.5 us -> 14.8 us  [per_device(): lax.all_to_all(mixed, 'sec', split_axis=0, concat_axis=0, tiled=True)]
    pallas_call x2, Pallas kernels: 7.76 us -> 3.59 us  [the longest x1 3.52 us: per_device(): pl.pallas_call(plane_kernel, out_shape=jax.ShapeDtypeStruct((groups, 5, l...]
    unnamed x6 -> x18, local copies, waits for them, and re-layouts: 0.63 us -> 2.54 us
    pallas_call x1, Pallas kernels: 2.15 us -> 0.39 us  [per_device(): pl.pallas_call(functools.partial(spread_kernel, layers, inner_rows, block...]
    ppermute x1, waiting for transfers between devices: 2.74 us -> 3.57 us  [per_device(): after = lax.ppermute(first, 'tile', down)]
    pallas_call x1, Pallas kernels: 2.34 us -> 1.66 us  [per_device(): pl.pallas_call(cross_kernel, out_shape=jax.ShapeDtypeStruct((2, groups *...]
  transfers between devices with their start and end apart: 2 -> 2, of which waited for: 1 -> 1; matrix products, arithmetic and copies ran while one was open for 0% -> 0% of each run, Pallas kernels for 5% -> 1%
where the time goes in v4:
time: 33.3 us; the launch traced here: 33 us
  blocking collectives  14.8 us (44%)
  starting transfers between devices  6.35 us (19%)
  Pallas kernels  5.64 us (17%)
  waiting for transfers between devices  3.57 us (11%)
  local copies, waits for them, and re-layouts  2.54 us (8%)
    all_to_all x1, blocking collectives, per_device(): lax.all_to_all(mixed, 'sec', split_axis=0, concat_axis=0, tiled=True)  14.8 us
    ppermute x1, starting transfers between devices, per_device(): before = lax.ppermute(last, 'tile', up)  5.06 us
    ppermute x1, waiting for transfers between devices, per_device(): after = lax.ppermute(first, 'tile', down)  3.57 us
    pallas_call x1, Pallas kernels, per_device(): pl.pallas_call(plane_kernel, out_shape=jax.ShapeDtypeStruct((groups, 5, l...  3.52 us
    unnamed x18, local copies, waits for them, and re-layouts  2.54 us
    pallas_call x1, Pallas kernels, per_device(): pl.pallas_call(cross_kernel, out_shape=jax.ShapeDtypeStruct((2, groups *...  1.66 us
    ppermute x1, starting transfers between devices, per_device(): after = lax.ppermute(first, 'tile', down)  1.29 us
  transfers between devices with their start and end apart: 2, of which 1 were waited for; matrix products, arithmetic and copies ran while one was open for 0% of the time, Pallas kernels for 1%

profile of v4, /device:TPU:0, one launch (start us, length us, event | category | flops | bytes accessed | tf_op | source)
XLA Modules:
  0.0 33.0 jit_solution(6352552056815182700)
XLA Ops:
  0.0 0.0 copy-start
  0.0 0.9 %copy-done = f32[2,2,64,256]{3,2,1,0:T(8,128)S(1)} copy-done((f32[2,2,64,256]{3,2,1,0:T(8,128)S(1)}, f32[2,2,64,256]{3,2,1,0:T(8,128)}, u32[]{:S(2)}) %copy-start) | copy-done | bytes 262168
  1.0 0.0 copy-start.2
  1.0 0.9 %copy-done.2 = f32[2,64,256]{2,1,0:T(8,128)S(1)} copy-done((f32[2,64,256]{2,1,0:T(8,128)S(1)}, f32[2,64,256]{2,1,0:T(8,128)}, u32[]{:S(2)}) %copy-start.2) | copy-done | bytes 131096
  1.9 0.0 copy-start.4
  1.9 0.0 copy-start.5
  1.9 0.1 pack_edges.1
  1.9 5.1 %collective-permute-start = (f32[3,2,8,256]{3,2,1,0:T(8,128)S(1)}, f32[3,2,8,256]{3,2,1,0:T(8,128)S(1)}, u32[]{:S(2)}, u32[]{:S(2)}) collective-permute-start(f32[3,2,8,256]{3,2,1,0:T(8,128)S(1)} %get-tuple-element.7), channel_id=1, source_target_pairs={{0,1},{1,2},{2,3},{4,5},{5,6},{6,7},{8,9},{9,10},{10,11},{12,13},{... | collective-permute-start | bytes 147464 | tf_op jit(solution)/shard_map/ppermute | solution.py:213
  7.0 1.3 %collective-permute-start.1 = (f32[3,2,8,256]{3,2,1,0:T(8,128)S(1)}, f32[3,2,8,256]{3,2,1,0:T(8,128)S(1)}, u32[]{:S(2)}, u32[]{:S(2)}) collective-permute-start(f32[3,2,8,256]{3,2,1,0:T(8,128)S(1)} %get-tuple-element.8), channel_id=1, source_target_pairs={{1,0},{2,1},{3,2},{5,4},{6,5},{7,6},{9,8},{10,9},{11,10},{13,12},{... | collective-permute-start | bytes 147464 | tf_op jit(solution)/shard_map/ppermute | solution.py:214
  8.3 0.0 copy-start.8
  8.3 0.0 copy-start.7
  8.3 0.0 copy-done.4
  8.3 0.0 copy-done.5
  8.4 0.6 %copy-done.8 = s32[1,1,256]{2,1,0:T(1,128)S(1)} copy-done((s32[1,1,256]{2,1,0:T(1,128)S(1)}, s32[1,1,256]{2,1,0:T(1,128)}, u32[]{:S(2)}) %copy-start.8) | copy-done | bytes 1048
  9.0 0.0 copy-done.7
  9.0 0.0 copy-start.1
  9.0 0.0 copy-start.3
  9.0 0.4 %spread_patches.1.forces_ref = f32[8,3,2,8,256]{4,3,2,1,0:T(8,128)S(1)} custom-call(s32[1,256]{1,0:T(1,128)S(1)} %bitcast.6, s32[1,256]{1,0:T(1,128)S(1)} %bitcast.7, f32[512,128]{1,0:T(8,128)S(1)} %bitcast.4, f32[256,128]{1,0:T(8,128)S(1)} %bitcast.5), custom_call_target="tpu_custom_call" | custom-call | flops 150994944 | bytes 800000 | tf_op jit(solution)/shard_map/spread_patches/pallas_call | solution.py:215
  9.4 0.0 collective-permute-done.before_ref
  9.4 3.6 %collective-permute-done.1.after_ref = f32[3,2,8,256]{3,2,1,0:T(8,128)S(1)} collective-permute-done((f32[3,2,8,256]{3,2,1,0:T(8,128)S(1)}, f32[3,2,8,256]{3,2,1,0:T(8,128)S(1)}, u32[]{:S(2)}, u32[]{:S(2)}) %collective-permute-start.1) | collective-permute-done | bytes 49184 | tf_op jit(solution)/shard_map/ppermute | solution.py:214
  13.0 0.0 copy-done.1
  13.0 0.0 copy-done.3
  13.0 3.5 %plane_steps.1 = f32[8,5,2,8,256]{4,3,2,1,0:T(8,128)S(1)} custom-call(f32[2,2,64,256]{3,2,1,0:T(8,128)S(1)} %copy-done.1, f32[2,64,256]{2,1,0:T(8,128)S(1)} %copy-done.3, f32[3,2,8,256]{3,2,1,0:T(8,128)S(1)} %collective-permute-done.before_ref, f32[3,2,8,256]{3,2,1,0:T(8,128)S(1)} %collective-permute-done.1.after_ref, ...), custom_call_target="tpu_custom_call" | custom-call | flops 10000000 | bytes 10000000 | tf_op jit(solution)/shard_map/plane_steps/pallas_call | solution.py:229
  16.5 0.0 copy-start.6
  16.5 14.8 %all_to_all.5.moved_ref = f32[8,5,2,8,256]{4,3,2,1,0:T(8,128)S(1)} all-to-all(f32[8,5,2,8,256]{4,3,2,1,0:T(8,128)S(1)} %plane_steps.1), channel_id=1, replica_groups=mesh['sec'=8,'tile'=4] {'sec'}, dimensions={0} | all-to-all | bytes 1310720 | tf_op jit(solution)/shard_map/all_to_all | solution.py:244
  31.3 0.0 copy-done.6
  31.3 1.7 %cross_steps.1 = f32[2,16,8,256]{3,2,1,0:T(8,128)} custom-call(f32[8,5,2,8,256]{4,3,2,1,0:T(8,128)S(1)} %all_to_all.5.moved_ref, f32[16,8,256]{2,1,0:T(8,128)S(1)} %copy-done.6), custom_call_target="tpu_custom_call" | custom-call | flops 10000000 | bytes 800000 | tf_op jit(solution)/shard_map/cross_steps/pallas_call | solution.py:245
Async XLA Ops:
  0.0 0.9 %copy-start = (f32[2,2,64,256]{3,2,1,0:T(8,128)S(1)}, f32[2,2,64,256]{3,2,1,0:T(8,128)}, u32[]{:S(2)}) copy-start(f32[2,2,64,256]{3,2,1,0:T(8,128)} %force_ref.3) | copy-start | bytes 786436
  1.0 0.9 %copy-start.2 = (f32[2,64,256]{2,1,0:T(8,128)S(1)}, f32[2,64,256]{2,1,0:T(8,128)}, u32[]{:S(2)}) copy-start(f32[2,64,256]{2,1,0:T(8,128)} %stiff_ref.4) | copy-start | bytes 393220
  1.9 6.5 %copy-start.4 = (f32[1,1,256,2,128]{4,3,2,1,0:T(2,128)S(1)}, f32[1,1,256,2,128]{4,3,2,1,0:T(2,128)}, u32[]{:S(2)}) copy-start(f32[1,1,256,2,128]{4,3,2,1,0:T(2,128)} %param.12) | copy-start | bytes 786436
  1.9 6.5 %copy-start.5 = (f32[1,1,256,128]{3,2,1,0:T(8,128)S(1)}, f32[1,1,256,128]{3,2,1,0:T(8,128)}, u32[]{:S(2)}) copy-start(f32[1,1,256,128]{3,2,1,0:T(8,128)} %param.13) | copy-start | bytes 393220
  1.9 7.5 %collective-permute-start = (f32[3,2,8,256]{3,2,1,0:T(8,128)S(1)}, f32[3,2,8,256]{3,2,1,0:T(8,128)S(1)}, u32[]{:S(2)}, u32[]{:S(2)}) collective-permute-start(f32[3,2,8,256]{3,2,1,0:T(8,128)S(1)} %get-tuple-element.7), channel_id=1, source_target_pairs={{0,1},{1,2},{2,3},{4,5},{5,6},{6,7},{8,9},{9,10},{10,11},{12,13},{... | collective-permute-start | bytes 147464 | tf_op jit(solution)/shard_map/ppermute | solution.py:213
  7.0 6.0 %collective-permute-start.1 = (f32[3,2,8,256]{3,2,1,0:T(8,128)S(1)}, f32[3,2,8,256]{3,2,1,0:T(8,128)S(1)}, u32[]{:S(2)}, u32[]{:S(2)}) collective-permute-start(f32[3,2,8,256]{3,2,1,0:T(8,128)S(1)} %get-tuple-element.8), channel_id=1, source_target_pairs={{1,0},{2,1},{3,2},{5,4},{6,5},{7,6},{9,8},{10,9},{11,10},{13,12},{... | collective-permute-start | bytes 147464 | tf_op jit(solution)/shard_map/ppermute | solution.py:214
  8.3 0.7 %copy-start.8 = (s32[1,1,256]{2,1,0:T(1,128)S(1)}, s32[1,1,256]{2,1,0:T(1,128)}, u32[]{:S(2)}) copy-start(s32[1,1,256]{2,1,0:T(1,128)} %param.11) | copy-start | bytes 3076
  8.3 0.7 %copy-start.7 = (s32[1,1,256,1]{2,3,1,0:T(1,128)S(1)}, s32[1,1,256,1]{2,3,1,0:T(1,128)}, u32[]{:S(2)}) copy-start(s32[1,1,256,1]{2,3,1,0:T(1,128)} %param.10) | copy-start | bytes 3076
  9.0 4.0 %copy-start.1 = (f32[2,2,64,256]{3,2,1,0:T(8,128)S(1)}, f32[2,2,64,256]{3,2,1,0:T(8,128)}, u32[]{:S(2)}) copy-start(f32[2,2,64,256]{3,2,1,0:T(8,128)} %force_ref.3) | copy-start | bytes 786436
  9.0 4.0 %copy-start.3 = (f32[2,64,256]{2,1,0:T(8,128)S(1)}, f32[2,64,256]{2,1,0:T(8,128)}, u32[]{:S(2)}) copy-start(f32[2,64,256]{2,1,0:T(8,128)} %stiff_ref.4) | copy-start | bytes 393220
  16.5 14.8 %copy-start.6 = (f32[16,8,256]{2,1,0:T(8,128)S(1)}, f32[16,8,256]{2,1,0:T(8,128)}, u32[]{:S(2)}) copy-start(f32[16,8,256]{2,1,0:T(8,128)} %stiff_ref.5) | copy-start | bytes 393220
